TPU v7x, 512 devices: a whole 4x8x8 slice. The times are simulated.
512 devices in a mesh: blocks: 64 (over y, z), octant: 8 (over x, core).
Axes of the slice: x: 4, y: 8, z: 8, core: 2. Of those that a mesh axis runs over, the one named last changes fastest.
Arguments:
- em_store: bfloat16 [8, 4096, 64], P('octant', 'blocks'), may hold values from 0 to 1, as said below
- route_block: int32 [8, 4096], P('octant', 'blocks'), may hold values from 0 to 63, as said below
- route_slot: int32 [8, 4096], P('octant', 'blocks'), may hold values from 0 to 63, as said below
- conv1_w: bfloat16 [32, 27], replicated, may hold values from -1.25 to 1.25
- conv1_b: float32 [32], replicated, may hold values from -3 to 3
- conv2_w: bfloat16 [27, 32, 32], replicated, may hold values from -0.21875 to 0.21875
- conv2_b: float32 [32], replicated, may hold values from -3 to 3
- head_w: bfloat16 [3, 32], replicated, may hold values from -1 to 1
- head_b: float32 [3], replicated, may hold values from -3 to 3
Outputs:
- affinities: float32 [8, 64, 3, 4096], P('octant', 'blocks')
Inputs may be any that keep to these rules, and one draw needn't show every extreme that they name: For each octant index, the pairs (route_block, route_slot) are all distinct, so every tile receives exactly 64 sub-blocks; the sub-blocks that one storage device sends to one tissue block are at most 2, and every storage device sends exactly 2 to some tissue block. `route_slot`: slot s lies at sub-block coordinates (s // 4 ** 2, s // 4 % 4, s % 4) of the tile. `em_store`: the tiles of one tissue block are cut from one volume of that block: where two tiles cover the same voxel they hold the same intensity.
All inputs are finite; a program needn't handle non-finite values.
Results may differ from a plain program's by a relative error of at most 0.002.
Values may be sent and summed in bfloat16 or wider, within the bound.
A program may use at most 64 MiB of HBM per device.

v0:
```python
import jax
import jax.numpy as jnp
from jax import lax
from jax.sharding import PartitionSpec as P

SB = 4
TS = 4
TILE = 16
OVL = 6
STEP = 10


def from_partner(value, axis, stride):
    mask = 2**stride
    pairs = [(source, source ^ mask) for source in range(lax.axis_size(axis))]
    return lax.ppermute(value, axis, pairs)


def padded_volume(volume, edge_len):
    reach_len = edge_len + 1
    return (jnp.pad(volume, ((0, 0), (1, 1), (reach_len, reach_len))), reach_len)


def window_at(padded, tap_index, edge_len, reach_len, row_of, col_of):
    shift_x = tap_index // 9
    shift_y = tap_index // 3 % 3 - 1
    shift_z = tap_index % 3 - 1
    plane_len = edge_len * edge_len
    offset = reach_len + shift_y * edge_len + shift_z
    window = padded[:, shift_x : shift_x + edge_len, offset : offset + plane_len]
    inside = (
        (row_of + shift_y >= 0)
        & (row_of + shift_y < edge_len)
        & (col_of + shift_z >= 0)
        & (col_of + shift_z < edge_len)
    )
    return window * inside.astype(window.dtype)


def shards(em_store, route_block, route_slot, conv1_w, conv1_b, conv2_w, conv2_b, head_w, head_b):
    blocks_count = lax.axis_size("blocks")
    stored = em_store.shape[1]
    capacity = max(2, stored // blocks_count)
    targets = route_block[0]
    places = route_slot[0]
    item_ids = jnp.arange(stored)
    earlier = (targets[:, None] == targets[None, :]) & (item_ids[None, :] < item_ids[:, None])
    item_ranks = jnp.sum(earlier.astype(jnp.int32), axis=1)
    buffer_rows = targets * capacity + item_ranks
    chosen = jnp.arange(blocks_count * capacity)[:, None] == buffer_rows[None, :]
    outgoing = jnp.dot(
        chosen.astype(jnp.bfloat16), em_store[0], preferred_element_type=jnp.float32
    ).astype(jnp.bfloat16)
    labels = jnp.sum(jnp.where(chosen, places[None, :] + 1, 0), axis=1) - 1
    arrived, arrived_labels = (
        lax.all_to_all(
            outgoing.reshape(blocks_count, capacity, -1),
            "blocks",
            split_axis=0,
            concat_axis=0,
            tiled=True,
        ),
        lax.all_to_all(
            labels.reshape(blocks_count, capacity),
            "blocks",
            split_axis=0,
            concat_axis=0,
            tiled=True,
        ),
    )
    picker = (jnp.arange(stored)[:, None] == arrived_labels.reshape(-1)[None, :]).astype(
        jnp.bfloat16
    )
    tile_em = jnp.dot(
        picker, arrived.reshape(blocks_count * capacity, -1), preferred_element_type=jnp.float32
    ).astype(jnp.bfloat16)
    edge_len = TILE
    plane_len = edge_len * edge_len
    volume = (
        tile_em.reshape(TS, TS, TS, SB, SB, SB)
        .transpose(0, 3, 1, 4, 2, 5)
        .reshape(1, edge_len, plane_len)
    )
    flat_ids = jnp.arange(plane_len)
    row_of = flat_ids // edge_len
    col_of = flat_ids % edge_len
    padded, reach_len = padded_volume(volume, edge_len)
    stacked = jnp.concatenate(
        [
            window_at(padded, tap_index, edge_len, reach_len, row_of, col_of)
            for tap_index in range(27)
        ],
        axis=0,
    )
    first_sum = jnp.einsum("ot,txp->oxp", conv1_w, stacked, preferred_element_type=jnp.float32)
    hidden_one = jax.nn.relu(first_sum + conv1_b[:, None, None]).astype(jnp.bfloat16)
    padded, reach_len = padded_volume(hidden_one, edge_len)
    second = jnp.zeros((conv2_w.shape[1], edge_len, plane_len), jnp.float32)
    for tap_index in range(27):
        window = window_at(padded, tap_index, edge_len, reach_len, row_of, col_of)
        second = second + jnp.einsum(
            "oc,cxp->oxp", conv2_w[tap_index], window, preferred_element_type=jnp.float32
        )
    hidden_two = jax.nn.relu(second + conv2_b[:, None, None]).astype(jnp.bfloat16)
    logits = (
        jnp.einsum("ac,cxp->axp", head_w, hidden_two, preferred_element_type=jnp.float32)
        + head_b[:, None, None]
    )
    predicted = jax.nn.sigmoid(logits)
    channels = predicted.shape[0]
    own_rank = lax.axis_index("octant")
    octant_count = lax.axis_size("octant")
    split_dims = octant_count.bit_length() - 1
    position = jnp.arange(edge_len, dtype=jnp.float32)
    lower_ramp = jnp.clip((edge_len - position - 0.5) / OVL, 0.0, 1.0)
    upper_ramp = jnp.clip((position + 0.5) / OVL, 0.0, 1.0)
    factors = []
    for axis_dim in range(3):
        own_bit = own_rank >> axis_dim & 1
        factors.append(jnp.where(own_bit == 1, upper_ramp, lower_ramp))
    weights = (
        factors[0][:, None]
        * (factors[1][:, None] * factors[2][None, :]).reshape(plane_len)[None, :]
    )
    blended = (predicted * weights[None]).reshape(channels, edge_len, edge_len, edge_len)
    summed = blended
    for axis_dim in range(split_dims):
        own_bit = own_rank >> axis_dim & 1
        start_at = (1 - own_bit) * STEP
        turned = jnp.moveaxis(summed, axis_dim + 1, 1)
        own_slab = lax.dynamic_slice_in_dim(turned, start_at, OVL, 1).reshape(
            channels, OVL, plane_len
        )
        partner = from_partner(own_slab, "octant", axis_dim)
        joined = (own_slab + partner).reshape(channels, OVL, edge_len, edge_len)
        turned = lax.dynamic_update_slice_in_dim(turned, joined, start_at, 1)
        summed = jnp.moveaxis(turned, 1, axis_dim + 1)
    return summed.reshape(1, 1, channels, edge_len * plane_len)


def solution(mesh):
    in_specs = (
        P("octant", "blocks", None),
        P("octant", "blocks"),
        P("octant", "blocks"),
        P(),
        P(),
        P(),
        P(),
        P(),
        P(),
    )
    out_specs = P("octant", "blocks", None, None)
    return jax.shard_map(shards, mesh=mesh, in_specs=in_specs, out_specs=out_specs, check_vma=False)
```

profile of v0, /device:TPU:1, one launch (start us, length us, event | category | flops | bytes accessed | tf_op | source)
XLA Modules:
  0.0 87.3 jit_solution(12290982455248813788)
XLA Ops:
  0.0 0.7 copy-done.4
  0.7 0.2 convert_reduce_fusion
  0.8 0.5 copy-done.5
  1.4 0.8 sub.141
  2.2 17.1 %all-to-all-start = ((s32[64,1,2]{2,1,0:T(1,128)}), s32[64,1,2]{2,1,0:T(1,128)S(1)}, u32[]{:S(2)}, u32[]{:S(2)}) async-start(s32[64,1,2]{2,1,0:T(1,128)} %bitcast.4), calls=%async_computation | async-start | bytes 65536 | tf_op jit(solution)/shard_map/all_to_all | solution.py:63
  19.6 0.2 convolution_convert_fusion.1
  19.9 0.7 copy.44
  20.6 9.6 %all-to-all-done = s32[64,1,2]{2,1,0:T(1,128)S(1)} async-done(((s32[64,1,2]{2,1,0:T(1,128)}), s32[64,1,2]{2,1,0:T(1,128)S(1)}, u32[]{:S(2)}, u32[]{:S(2)}) %all-to-all-start) | async-done | bytes 544 | tf_op jit(solution)/shard_map/all_to_all | solution.py:63
  30.2 4.6 %all-to-all-start.1 = ((bf16[64,2,64]{2,1,0:T(2,128)(2,1)}), bf16[64,2,64]{2,1,0:T(2,128)(2,1)S(1)}, u32[]{:S(2)}, u32[]{:S(2)}) async-start(bf16[64,2,64]{2,1,0:T(2,128)(2,1)} %bitcast.6), calls=%async_computation.1 | async-start | bytes 65536 | tf_op jit(solution)/shard_map/all_to_all | solution.py:56
  34.8 0.6 broadcast.617
  35.4 0.8 reduce.3
  36.2 0.1 eq.65
  36.3 9.2 %all-to-all-done.1 = bf16[64,2,64]{2,1,0:T(2,128)(2,1)S(1)} async-done(((bf16[64,2,64]{2,1,0:T(2,128)(2,1)}), bf16[64,2,64]{2,1,0:T(2,128)(2,1)S(1)}, u32[]{:S(2)}, u32[]{:S(2)}) %all-to-all-start.1) | async-done | bytes 16416 | tf_op jit(solution)/shard_map/all_to_all | solution.py:56
  45.5 0.1 convolution_convert_fusion
  45.7 0.3 reshape.195
  46.1 0.3 reshape.235
  46.5 0.3 slice_multiply_fusion.2
  46.8 0.3 slice_multiply_fusion.1
  47.1 0.3 slice_multiply_fusion
  47.3 0.3 slice_multiply_fusion.3
  47.6 0.7 concatenate.3
  48.3 0.2 fusion.17
  48.5 0.7 copy-done.1
  49.2 0.3 fusion.26
  49.5 0.3 convolution_add_fusion.15
  49.8 0.3 convolution_add_fusion.14
  50.1 0.3 convolution_add_fusion.13
  50.4 0.2 convolution_add_fusion.12
  50.6 0.3 convolution_add_fusion.11
  50.9 0.3 convolution_add_fusion.10
  51.2 0.3 convolution_add_fusion.9
  51.5 0.3 convolution_add_fusion.8
  51.8 0.3 convolution_add_fusion.7
  52.1 0.3 convolution_add_fusion.6
  52.4 0.3 convolution_add_fusion.5
  52.6 0.3 convolution_add_fusion.4
  52.9 0.2 convolution_add_fusion.3
  53.2 0.3 convolution_add_fusion.2
  53.5 0.3 convolution_add_fusion.1
  53.8 0.3 fusion.10
  54.0 0.3 fusion.9
  54.3 0.3 fusion.8
  54.6 0.3 fusion.7
  54.9 0.3 fusion.6
  55.2 0.3 fusion.5
  55.5 0.2 fusion.4
  55.7 0.3 fusion.3
  56.0 0.3 fusion.2
  56.4 0.3 fusion.1
  56.7 0.4 copy-done.6
  57.0 0.4 fusion.24
  57.5 0.2 reshape.197
  57.8 5.1 %collective-permute-start = (f32[3,6,256]{2,1,0:T(8,128)S(1)}, f32[3,6,256]{2,1,0:T(8,128)S(1)}, u32[]{:S(2)}, u32[]{:S(2)}) collective-permute-start(f32[3,6,256]{2,1,0:T(8,128)S(1)} %reshape.198), channel_id=1, source_target_pairs={{0,1},{1,0},{2,3},{3,2},{4,5},{5,4},{6,7},{7,6},{8,9},{9,8},{10,11... | collective-permute-start | bytes 55304 | tf_op jit(solution)/shard_map/ppermute | solution.py:16
  62.9 0.8 collective-permute-done
  64.1 3.1 %collective-permute-start.1 = (f32[3,6,256]{2,1,0:T(8,128)S(1)}, f32[3,6,256]{2,1,0:T(8,128)S(1)}, u32[]{:S(2)}, u32[]{:S(2)}) collective-permute-start(f32[3,6,256]{2,1,0:T(8,128)S(1)} %reshape.200), channel_id=1, source_target_pairs={{0,2},{1,3},{2,0},{3,1},{4,6},{5,7},{6,4},{7,5},{8,10},{9,11},{10,... | collective-permute-start | bytes 55304 | tf_op jit(solution)/shard_map/ppermute | solution.py:16
  67.2 1.4 %collective-permute-done.1 = f32[3,6,256]{2,1,0:T(8,128)S(1)} collective-permute-done((f32[3,6,256]{2,1,0:T(8,128)S(1)}, f32[3,6,256]{2,1,0:T(8,128)S(1)}, u32[]{:S(2)}, u32[]{:S(2)}) %collective-permute-start.1) | collective-permute-done | bytes 18464 | tf_op jit(solution)/shard_map/ppermute | solution.py:16
  68.8 0.2 dynamic_update_slice.10
  69.1 0.2 constant_dynamic-slice_fusion
  69.2 0.2 copy.54
  69.4 4.7 %collective-permute-start.2 = (f32[3,6,256]{2,1,0:T(8,128)S(1)}, f32[3,6,256]{2,1,0:T(8,128)S(1)}, u32[]{:S(2)}, u32[]{:S(2)}) collective-permute-start(f32[3,6,256]{2,1,0:T(8,128)S(1)} %copy.54), channel_id=1, source_target_pairs={{0,4},{1,5},{2,6},{3,7},{4,0},{5,1},{6,2},{7,3},{8,12},{9,13},{10,... | collective-permute-start | bytes 55304 | tf_op jit(solution)/shard_map/ppermute | solution.py:16
  74.1 1.4 %collective-permute-done.2 = f32[3,6,256]{2,1,0:T(8,128)S(1)} collective-permute-done((f32[3,6,256]{2,1,0:T(8,128)S(1)}, f32[3,6,256]{2,1,0:T(8,128)S(1)}, u32[]{:S(2)}, u32[]{:S(2)}) %collective-permute-start.2) | collective-permute-done | bytes 18464 | tf_op jit(solution)/shard_map/ppermute | solution.py:16
  75.5 0.2 copy.55
  75.7 10.9 %dynamic_update_slice.11 = f32[3,16,16,16]{1,3,2,0:T(8,128)S(1)} dynamic-update-slice(f32[3,16,16,16]{1,3,2,0:T(8,128)S(1)} %bitcast.219, f32[3,6,16,16]{1,3,2,0:T(8,128)S(1)} %bitcast.221, s32[]{:T(128)} %constant.75.clone.1, s32[]{:T(128)S(6)} %select_n.319, s32[]{:T(128)} %constant.75.clone.1, s32[]{:T(128)} %constant.75.clone.1) | dynamic-update-slice | bytes 36868 | tf_op jit(solution)/shard_map/dynamic_update_slice | solution.py:136
  86.5 0.8 reshape.234
  (42 shorter events, 1.2 us)
Async XLA Ops:
  0.0 19.6 %copy-start = (bf16[1,64,64]{2,1,0:T(8,128)(2,1)S(1)}, bf16[1,64,64]{2,1,0:T(8,128)(2,1)}, u32[]{:S(2)}) copy-start(bf16[1,64,64]{2,1,0:T(8,128)(2,1)} %param.9) | copy-start | bytes 24580
  0.0 0.7 copy-start.4
  0.7 0.7 copy-start.5
  2.2 28.0 %all-to-all-start = ((s32[64,1,2]{2,1,0:T(1,128)}), s32[64,1,2]{2,1,0:T(1,128)S(1)}, u32[]{:S(2)}, u32[]{:S(2)}) async-start(s32[64,1,2]{2,1,0:T(1,128)} %bitcast.4), calls=%async_computation | async-start | bytes 65536 | tf_op jit(solution)/shard_map/all_to_all | solution.py:63
  30.2 15.3 %all-to-all-start.1 = ((bf16[64,2,64]{2,1,0:T(2,128)(2,1)}), bf16[64,2,64]{2,1,0:T(2,128)(2,1)S(1)}, u32[]{:S(2)}, u32[]{:S(2)}) async-start(bf16[64,2,64]{2,1,0:T(2,128)(2,1)} %bitcast.6), calls=%async_computation.1 | async-start | bytes 65536 | tf_op jit(solution)/shard_map/all_to_all | solution.py:56
  47.6 0.7 copy-start.2
  47.6 0.7 copy-start.3
  48.3 0.9 %copy-start.1 = (bf16[27,32,32]{2,1,0:T(8,128)(2,1)S(1)}, bf16[27,32,32]{2,1,0:T(8,128)(2,1)}, u32[]{:S(2)}) copy-start(bf16[27,32,32]{2,1,0:T(8,128)(2,1)} %param.14) | copy-start | bytes 165892
  56.3 0.7 copy-start.6
  56.3 0.7 copy-start.7
  56.4 0.7 copy-start.8
  57.8 6.0 %collective-permute-start = (f32[3,6,256]{2,1,0:T(8,128)S(1)}, f32[3,6,256]{2,1,0:T(8,128)S(1)}, u32[]{:S(2)}, u32[]{:S(2)}) collective-permute-start(f32[3,6,256]{2,1,0:T(8,128)S(1)} %reshape.198), channel_id=1, source_target_pairs={{0,1},{1,0},{2,3},{3,2},{4,5},{5,4},{6,7},{7,6},{8,9},{9,8},{10,11... | collective-permute-start | bytes 55304 | tf_op jit(solution)/shard_map/ppermute | solution.py:16
  64.1 4.6 %collective-permute-start.1 = (f32[3,6,256]{2,1,0:T(8,128)S(1)}, f32[3,6,256]{2,1,0:T(8,128)S(1)}, u32[]{:S(2)}, u32[]{:S(2)}) collective-permute-start(f32[3,6,256]{2,1,0:T(8,128)S(1)} %reshape.200), channel_id=1, source_target_pairs={{0,2},{1,3},{2,0},{3,1},{4,6},{5,7},{6,4},{7,5},{8,10},{9,11},{10,... | collective-permute-start | bytes 55304 | tf_op jit(solution)/shard_map/ppermute | solution.py:16
  69.4 6.1 %collective-permute-start.2 = (f32[3,6,256]{2,1,0:T(8,128)S(1)}, f32[3,6,256]{2,1,0:T(8,128)S(1)}, u32[]{:S(2)}, u32[]{:S(2)}) collective-permute-start(f32[3,6,256]{2,1,0:T(8,128)S(1)} %copy.54), channel_id=1, source_target_pairs={{0,4},{1,5},{2,6},{3,7},{4,0},{5,1},{6,2},{7,3},{8,12},{9,13},{10,... | collective-permute-start | bytes 55304 | tf_op jit(solution)/shard_map/ppermute | solution.py:16
where the time goes:
time: 88.9 us; the launch traced here: 87.3 us
  starting transfers between devices  34.6 us (39%)
  waiting for transfers between devices  22.5 us (25%)
  local copies, waits for them, and re-layouts  19.1 us (21%)
  matrix products  8.19 us (9%)
  other arithmetic  2.4 us (3%)
    all_to_all x1, starting transfers between devices, shards(): lax.all_to_all(labels.reshape(blocks_count, capacity), 'blocks', split_ax...  17.1 us
    ppermute x3, starting transfers between devices, from_partner(): return lax.ppermute(value, axis, pairs)  12.9 us
    dynamic_update_slice x3, local copies, waits for them, and re-layouts, shards(): turned = lax.dynamic_update_slice_in_dim(turned, joined, start_at, 1)  11.1 us
    all_to_all x1, waiting for transfers between devices, shards(): lax.all_to_all(labels.reshape(blocks_count, capacity), 'blocks', split_ax...  9.57 us
    all_to_all x1, waiting for transfers between devices, shards(): lax.all_to_all(outgoing.reshape(blocks_count, capacity, -1), 'blocks', sp...  9.23 us
    dot_general x26, matrix products, shards(): jnp.einsum('oc,cxp->oxp', conv2_w[tap_index], window, preferred_element_t...  7.21 us
    all_to_all x1, starting transfers between devices, shards(): lax.all_to_all(outgoing.reshape(blocks_count, capacity, -1), 'blocks', sp...  4.59 us
    ppermute x3, waiting for transfers between devices, from_partner(): return lax.ppermute(value, axis, pairs)  3.68 us
  transfers between devices with their start and end apart: 5, of which 5 were waited for; matrix products, arithmetic and copies ran while one was open for 3% of the time, Pallas kernels for 0%

commit v1 on v0

v1 whole, which is shorter than its diff:
```python
import jax
import jax.numpy as jnp
from jax import lax
from jax.experimental import pallas as pl
from jax.experimental.pallas import tpu as pltpu
from jax.sharding import PartitionSpec as P

TILE = 16
OVL = 6
LANES = TILE * TILE
C1 = 32
AFF = 3
MESH = pl.DeviceIdType.MESH
F32 = jnp.float32
BF16 = jnp.bfloat16


def iota(shape, dim):
    return lax.broadcasted_iota(jnp.int32, shape, dim)


def dot(a, b):
    return jnp.dot(a, b, preferred_element_type=F32)


def column(row):
    n = row.shape[1]
    return jnp.sum(jnp.where(iota((n, n), 0) == iota((n, n), 1), row, 0.0), axis=1, keepdims=True)


def pack_rows(em, targets, slots):
    n = em.shape[0]
    target_row = targets.astype(F32)
    target_col = column(target_row)
    earlier = (target_col == target_row) & (iota((n, n), 0) < iota((n, n), 1))
    rank_row = jnp.sum(jnp.where(earlier, 1.0, 0.0), axis=0, keepdims=True)
    slot_row = slots
    i_col = column((slot_row // 16 + 1).astype(F32))
    jk_col = column((slot_row % 16).astype(F32))
    lane = iota((n, 128), 1)
    spread = iota((64, 128), 0) == iota((64, 128), 1)
    wide = dot(em, spread.astype(F32).astype(BF16))
    wide = jnp.where(lane == 64, i_col, jnp.where(lane == 65, jk_col, wide)).astype(BF16)
    here = iota((64, n), 0).astype(F32) == target_row
    parts = [
        dot((here & (rank_row == rank)).astype(F32).astype(BF16), wide) for rank in (0.0, 1.0)
    ]
    return jnp.concatenate(parts, axis=1)


def expander():
    row = iota((128, 4 * LANES), 0)
    col = iota((128, 4 * LANES), 1)
    wanted = (col // LANES) * 16 + (col // 16 % 4) * 4 + col % 4
    return (row == wanted).astype(F32).astype(BF16)


def unpack_volume(arrived, expand):
    rows = jnp.concatenate([arrived[:, :128], arrived[:, 128:]], axis=0)
    i_col = rows[:, 64:65]
    jk_col = rows[:, 65:66]
    eye = iota((128, 128), 0) == iota((128, 128), 1)
    i_row = jnp.sum(jnp.where(eye, i_col, 0.0), axis=0, keepdims=True)
    lane = iota((128, LANES), 1)
    lane_jk = (lane // 64 * 4 + lane // 4 % 4).astype(F32)
    inside = lane_jk == jk_col
    spread = dot(rows.astype(BF16), expand)
    x_row = iota((TILE, 128), 0)
    volume = jnp.zeros((TILE, LANES), F32)
    for a in range(4):
        masked = jnp.where(inside, spread[:, a * LANES : (a + 1) * LANES], 0.0).astype(BF16)
        wanted = (x_row % 4 == a) & ((x_row // 4 + 1).astype(F32) == i_row)
        volume = volume + dot(wanted.astype(F32).astype(BF16), masked)
    return volume


def first_matrix(conv1_w):
    tap = iota((27, LANES), 0)
    col = iota((27, LANES), 1)
    x_in = iota((TILE, C1, LANES), 2) % TILE
    x_out = iota((TILE, C1, LANES), 0)
    total = jnp.zeros((TILE, C1, LANES), F32)
    for dx in range(3):
        spread = ((tap == 9 * dx + col // TILE) & (col < 9 * TILE)).astype(F32).astype(BF16)
        rows = dot(conv1_w, spread)
        total = jnp.where(x_in == x_out + dx - 1, rows[None], total)
    return total.reshape(TILE * C1, LANES).astype(BF16)


def replicated(weights, count):
    shape = (C1, count * C1)
    return dot(weights, (iota(shape, 0) == iota(shape, 1) % C1).astype(F32).astype(BF16))


def shift_lanes(value, by, roll):
    return roll(value, (-by) % value.shape[-1], value.ndim - 1)


def conv1_columns(volume, roll):
    lane = iota((TILE, LANES), 1)
    y, z = lane // TILE, lane % TILE
    rows = []
    for dy in (-1, 0, 1):
        for dz in (-1, 0, 1):
            moved = volume
            if dy or dz:
                moved = shift_lanes(volume, dy * TILE + dz, roll)
                keep = (y + dy >= 0) & (y + dy < TILE) & (z + dz >= 0) & (z + dz < TILE)
                moved = jnp.where(keep, moved, 0.0)
            rows.append(moved)
    rows.append(jnp.zeros((LANES - 9 * TILE, LANES), F32))
    return jnp.concatenate(rows, axis=0).astype(BF16)


def z_shifted(half, roll):
    z = iota(half.shape, 1) % TILE
    before = jnp.where(z > 0, shift_lanes(half, -1, roll), 0.0)
    after = jnp.where(z < TILE - 1, shift_lanes(half, 1, roll), 0.0)
    return jnp.concatenate([before, half, after], axis=0).astype(BF16)


def head_matrix(head_w):
    wide = replicated(head_w, TILE)
    x_in = iota((TILE, TILE * C1), 1) // C1
    x_out = iota((TILE, TILE * C1), 0)
    rows = [jnp.where(x_in == x_out, wide[a : a + 1], 0.0) for a in range(AFF)]
    return jnp.concatenate(rows, axis=0).astype(BF16)


def ramp(position, bit):
    lower = jnp.minimum((TILE - position - 0.5) / OVL, 1.0)
    upper = jnp.minimum((position + 0.5) / OVL, 1.0)
    return jnp.where(bit == 1, upper, lower)


def blend_weights(bits):
    lane = iota((TILE, LANES), 1)
    x = iota((TILE, LANES), 0).astype(F32)
    y = (lane // TILE).astype(F32)
    z = (lane % TILE).astype(F32)
    return ramp(x, bits[0]) * (ramp(y, bits[1]) * ramp(z, bits[2]))


def move_x(low, high, bit, roll):
    row = iota(low.shape, 1)
    from_high = jnp.where(row < OVL, roll(high, 6, 1), 0.0)
    from_low = jnp.where(row >= 8 - OVL, roll(low, 2, 1), 0.0)
    return jnp.where(bit == 0, from_high, from_low)


def move_y(low, high, bit, roll):
    lane = iota(low.shape, 2)
    from_high = jnp.where(lane < OVL * TILE, roll(high, 96, 2), 0.0)
    from_low = jnp.where(lane >= 128 - OVL * TILE, roll(low, 32, 2), 0.0)
    return jnp.where(bit == 0, from_high, from_low)


def pack_z(first, second, bit, roll):
    z = iota(first.shape, 2) % TILE
    head = jnp.where(bit == 0, roll(first, 128 - 10, 2), first)
    tail = jnp.where(bit == 0, roll(second, 128 - 2, 2), roll(second, 8, 2))
    return jnp.where(z < 8, head, tail)


def unpack_z(packed, bit, roll):
    z = iota(packed.shape, 2) % TILE
    keep = jnp.where(bit == 0, z - 10, 5 - z) >= 0
    head = jnp.where(bit == 0, roll(packed, 10, 2), packed)
    tail = jnp.where(bit == 0, roll(packed, 2, 2), roll(packed, 128 - 8, 2))
    return jnp.where(keep, head, 0.0), jnp.where(keep, tail, 0.0)


def kernel(
    em_ref, block_ref, slot_ref, w1_ref, b1_ref, w2_ref, b2_ref, wh_ref, bh_ref,
    out_ref,
    em, block, slot, w1, b1, w2, b2, wh, bh,
    sent, arrived, expand, first, second, heads, hidden, partial,
    x_out, y_out, z_out, e_out, x_in, y_in, z_in, e_in,
    load_sems, route_send, route_recv, swap_send, swap_recv,
):
    roll = pltpu.roll
    blocks = 64
    me = lax.axis_index("blocks")
    own = lax.axis_index("octant")
    bits = [own % 2, own // 2 % 2, own // 4]

    def partner(mask):
        total = 0
        for d in range(3):
            total = total + (1 - bits[d] if mask >> d & 1 else bits[d]) * 2**d
        return total

    barrier = pltpu.get_barrier_semaphore()

    def greet(step, carry):
        pl.semaphore_signal(
            barrier, inc=1, device_id={"blocks": (me + step) % blocks}, device_id_type=MESH
        )
        return carry

    lax.fori_loop(1, blocks, greet, 0)
    for mask in range(1, 8):
        pl.semaphore_signal(
            barrier, inc=1, device_id={"octant": partner(mask)}, device_id_type=MESH
        )

    loads = [
        pltpu.make_async_copy(source, target, load_sems.at[index])
        for index, (source, target) in enumerate(
            [
                (em_ref, em), (block_ref, block), (slot_ref, slot),
                (w1_ref, w1), (b1_ref, b1), (w2_ref, w2), (b2_ref, b2), (wh_ref, wh), (bh_ref, bh),
            ]
        )
    ]
    for load in loads:
        load.start()
    for load in loads[:3]:
        load.wait()
    packed = pack_rows(em[0], block[...], slot[...])
    sent[:, 0, :] = packed
    pl.semaphore_wait(barrier, blocks - 1 + 7)

    def send(step, carry):
        target = (me + step) % blocks
        pltpu.make_async_remote_copy(
            src_ref=sent.at[target],
            dst_ref=arrived.at[me],
            send_sem=route_send,
            recv_sem=route_recv,
            device_id={"blocks": target},
            device_id_type=MESH,
        ).start()
        return carry

    lax.fori_loop(1, blocks, send, 0)
    arrived[me] = sent[me]

    for load in loads[3:]:
        load.wait()
    expand[...] = expander()
    first[...] = first_matrix(w1[...])
    wide = replicated(w2[...].reshape(27 * C1, C1), 8)
    x_inner = iota((C1, 8 * C1), 1) // C1
    for x in range(10):
        for dy in range(3):
            for dz in range(3):
                block_rows = jnp.zeros((C1, 8 * C1), F32)
                for dx in range(3):
                    if 0 <= x + dx - 2 < 8:
                        at = (9 * dx + 3 * dy + dz) * C1
                        block_rows = jnp.where(
                            x_inner == x + dx - 2, wide[at : at + C1], block_rows
                        )
                at = (x * 3 + dy) * C1
                second[at : at + C1, dz * 256 : dz * 256 + 256] = block_rows.astype(BF16)
    heads[...] = head_matrix(wh[...])
    b1_col = column(b1[...])
    b2_col = column(b2[...])
    weights = blend_weights(bits)

    whole = pltpu.make_async_remote_copy(
        src_ref=sent.at[pl.ds(0, blocks - 1)],
        dst_ref=arrived.at[pl.ds(0, blocks - 1)],
        send_sem=route_send,
        recv_sem=route_recv,
        device_id={"blocks": (me + 1) % blocks},
        device_id_type=MESH,
    )
    whole.wait_recv()
    volume = unpack_volume(arrived[:, 0, :], expand[...])
    one = dot(first[...], conv1_columns(volume, roll)).reshape(TILE, C1, LANES)
    one = jnp.maximum(one + b1_col[None], 0.0).reshape(TILE * C1, LANES)
    for h in range(2):
        hidden[h] = z_shifted(one[h * 256 : h * 256 + 256], roll)
    low = dot(second[3 * C1 : 30 * C1], hidden[0]).reshape(9, 3, C1, LANES)
    high = dot(second[: 27 * C1], hidden[1]).reshape(9, 3, C1, LANES)
    both = low[7:] + high[:2]
    partial[:7] = low[:7]
    partial[7:9] = both
    partial[9:] = high[2:]
    y = iota((1, 1, LANES), 2) // TILE
    total = partial[:, 1]
    total = total + jnp.where(y > 0, shift_lanes(partial[:, 0].reshape(512, LANES), -TILE, roll).reshape(TILE, C1, LANES), 0.0)
    total = total + jnp.where(y < TILE - 1, shift_lanes(partial[:, 2].reshape(512, LANES), TILE, roll).reshape(TILE, C1, LANES), 0.0)
    two = jnp.maximum(total + b2_col[None], 0.0).reshape(TILE * C1, LANES).astype(BF16)
    logits = dot(heads[...], two)
    pieces = []
    for a in range(AFF):
        pieces.append(jax.nn.sigmoid(logits[a * TILE : a * TILE + TILE] + bh[:, a : a + 1]) * weights)
    blended = jnp.stack(pieces, axis=0)

    tile = [[blended[:, 8 * hx : 8 * hx + 8, 128 * hy : 128 * hy + 128] for hy in range(2)] for hx in range(2)]
    at_x = [move_x(tile[0][hy], tile[1][hy], bits[0], roll) for hy in range(2)]
    at_y = [move_y(tile[hx][0], tile[hx][1], bits[1], roll) for hx in range(2)]
    at_xy = move_y(at_x[0], at_x[1], bits[1], roll)
    z_out[:, :8] = pack_z(tile[0][0], tile[0][1], bits[2], roll)
    z_out[:, 8:] = pack_z(tile[1][0], tile[1][1], bits[2], roll)
    x_out[:, :, :128] = at_x[0]
    x_out[:, :, 128:] = at_x[1]
    y_out[:, :8] = at_y[0]
    y_out[:, 8:] = at_y[1]
    e_out[0] = at_xy
    e_out[1] = pack_z(at_x[0], at_x[1], bits[2], roll)
    e_out[2] = pack_z(at_y[0], at_y[1], bits[2], roll)
    e_out[3] = pack_z(at_xy, at_xy, bits[2], roll)

    pairs = [
        (4, z_out, z_in), (2, y_out, y_in), (6, e_out.at[2], e_in.at[2]), (7, e_out.at[3], e_in.at[3]),
        (5, e_out.at[1], e_in.at[1]), (3, e_out.at[0], e_in.at[0]), (1, x_out, x_in),
    ]
    swaps = [
        pltpu.make_async_remote_copy(
            src_ref=source,
            dst_ref=target,
            send_sem=swap_send.at[mask - 1],
            recv_sem=swap_recv.at[mask - 1],
            device_id={"octant": partner(mask)},
            device_id_type=MESH,
        )
        for mask, source, target in pairs
    ]
    for swap in swaps:
        swap.start()
    for swap in swaps:
        swap.wait_recv()

    plane = [[tile[hx][hy] for hy in range(2)] for hx in range(2)]

    def add(hx, hy, value):
        plane[hx][hy] = plane[hx][hy] + value

    def is_half(bit, half, value):
        return jnp.where(bit == 1 - half, value, 0.0)

    for hy in range(2):
        value = x_in[:, :, 128 * hy : 128 * hy + 128]
        for hx in range(2):
            add(hx, hy, is_half(bits[0], hx, value))
    for hx in range(2):
        value = y_in[:, 8 * hx : 8 * hx + 8]
        for hy in range(2):
            add(hx, hy, is_half(bits[1], hy, value))
        parts = unpack_z(z_in[:, 8 * hx : 8 * hx + 8], bits[2], roll)
        for hy in range(2):
            add(hx, hy, parts[hy])
    corner = e_in[0] + unpack_z(e_in[3], bits[2], roll)[0]
    for hx in range(2):
        for hy in range(2):
            add(hx, hy, is_half(bits[0], hx, is_half(bits[1], hy, corner)))
    parts = unpack_z(e_in[1], bits[2], roll)
    for hx in range(2):
        for hy in range(2):
            add(hx, hy, is_half(bits[0], hx, parts[hy]))
    parts = unpack_z(e_in[2], bits[2], roll)
    for hx in range(2):
        for hy in range(2):
            add(hx, hy, is_half(bits[1], hy, parts[hx]))
    for hx in range(2):
        for hy in range(2):
            out_ref[:, 8 * hx : 8 * hx + 8, 128 * hy : 128 * hy + 128] = plane[hx][hy]
    for swap in swaps:
        swap.wait_send()
    whole.wait_send()


def shards(em_store, route_block, route_slot, conv1_w, conv1_b, conv2_w, conv2_b, head_w, head_b):
    operands = (
        em_store, route_block, route_slot, conv1_w, conv1_b.reshape(1, C1), conv2_w,
        conv2_b.reshape(1, C1), head_w, head_b.reshape(1, AFF),
    )
    vmem = pltpu.VMEM
    result = pl.pallas_call(
        kernel,
        out_shape=jax.ShapeDtypeStruct((AFF, TILE, LANES), F32),
        in_specs=[pl.BlockSpec(memory_space=pl.ANY)] * len(operands),
        out_specs=pl.BlockSpec(memory_space=vmem),
        scratch_shapes=[vmem(value.shape, value.dtype) for value in operands]
        + [
            vmem((64, 1, 256), F32),
            vmem((64, 1, 256), F32),
            vmem((128, 4 * LANES), BF16),
            vmem((TILE * C1, LANES), BF16),
            vmem((30 * C1, 3 * 256), BF16),
            vmem((AFF * TILE, TILE * C1), BF16),
            vmem((2, 768, LANES), BF16),
            vmem((TILE, 3, C1, LANES), F32),
        ]
        + [
            vmem((AFF, 8, 256), F32),
            vmem((AFF, 16, 128), F32),
            vmem((AFF, 16, 128), F32),
            vmem((4, AFF, 8, 128), F32),
        ]
        * 2
        + [
            pltpu.SemaphoreType.DMA((len(operands),)),
            pltpu.SemaphoreType.DMA,
            pltpu.SemaphoreType.DMA,
            pltpu.SemaphoreType.DMA((7,)),
            pltpu.SemaphoreType.DMA((7,)),
        ],
        compiler_params=pltpu.CompilerParams(
            collective_id=0, has_side_effects=True, vmem_limit_bytes=32 * 1024 * 1024
        ),
    )(*operands)
    return result.reshape(1, 1, AFF, TILE * LANES)


def solution(mesh):
    in_specs = (P("octant", "blocks", None), P("octant", "blocks"), P("octant", "blocks")) + (P(),) * 6
    out_specs = P("octant", "blocks", None, None)
    return jax.shard_map(shards, mesh=mesh, in_specs=in_specs, out_specs=out_specs, check_vma=False)
```

time: 88.9 us -> 33.8 us (0.38); the launches traced: 87.3 us -> 33.6 us
  starting transfers between devices: 34.6 us -> 0 us
  Pallas kernels: 0 us -> 29.8 us
  waiting for transfers between devices: 22.5 us -> 0 us
  local copies, waits for them, and re-layouts: 19.1 us -> 3.73 us
  matrix products: 8.19 us -> 0 us
  other arithmetic: 2.4 us -> 0 us
    pallas_call x0 -> x1, Pallas kernels: none -> 29.8 us  [shards(): pl.pallas_call(kernel, out_shape=jax.ShapeDtypeStruct((AFF, TILE, LANES),...]
    all_to_all x2 -> x0, starting transfers between devices: 21.7 us -> none  [the longest x1 17.1 us: shards(): lax.all_to_all(labels.reshape(blocks_count, capacity), 'blocks', split_ax...]
    all_to_all x2 -> x0, waiting for transfers between devices: 18.8 us -> none  [the longest x1 9.57 us: shards(): lax.all_to_all(labels.reshape(blocks_count, capacity), 'blocks', split_ax...]
    ppermute x3 -> x0, starting transfers between devices: 12.9 us -> none  [from_partner(): return lax.ppermute(value, axis, pairs)]
    dynamic_update_slice x3 -> x0, local copies, waits for them, and re-layouts: 11.1 us -> none  [shards(): turned = lax.dynamic_update_slice_in_dim(turned, joined, start_at, 1)]
    dot_general x30 -> x0, matrix products: 8.19 us -> none  [the longest x26 7.21 us: shards(): jnp.einsum('oc,cxp->oxp', conv2_w[tap_index], window, preferred_element_t...]
    ppermute x3 -> x0, waiting for transfers between devices: 3.68 us -> none  [from_partner(): return lax.ppermute(value, axis, pairs)]
    reshape x12 -> x1, local copies, waits for them, and re-layouts: 2.55 us -> 0.67 us  [shards(): return result.reshape(1, 1, AFF, TILE * LANES)]
  transfers between devices with their start and end apart: 5 -> 0, of which waited for: 5 -> 0; matrix products, arithmetic and copies ran while one was open for 3% -> 0% of each run, Pallas kernels for 0% -> 0%
where the time goes in v1:
time: 33.8 us; the launch traced here: 33.6 us
  Pallas kernels  29.8 us (88%)
  local copies, waits for them, and re-layouts  3.73 us (11%)
    pallas_call x1, Pallas kernels, shards(): pl.pallas_call(kernel, out_shape=jax.ShapeDtypeStruct((AFF, TILE, LANES),...  29.8 us
    unnamed x18, local copies, waits for them, and re-layouts  3.06 us

profile of v1, /device:TPU:1, one launch (start us, length us, event | category | flops | bytes accessed | tf_op | source)
XLA Modules:
  0.0 33.6 jit_solution(7374711176595443135)
XLA Ops:
  0.0 0.0 copy-start.5
  0.0 0.0 copy-start.6
  0.0 0.0 copy-start.7
  0.0 0.0 copy-start.8
  0.0 0.0 copy-start.3
  0.0 0.0 copy-start.4
  0.0 0.6 %copy-done.5 = s32[1,64]{1,0:T(1,128)S(1)} copy-done((s32[1,64]{1,0:T(1,128)S(1)}, s32[1,64]{1,0:T(1,128)}, u32[]{:S(2)}) %copy-start.5) | copy-done | bytes 280
  0.7 0.0 copy-done.6
  0.7 0.0 copy-done.7
  0.7 0.0 copy-done.8
  0.7 0.0 copy-done.3
  0.7 0.0 copy-done.4
  0.7 0.0 copy-start
  0.7 0.9 %copy-done = bf16[27,32,32]{2,1,0:T(8,128)(2,1)S(1)} copy-done((bf16[27,32,32]{2,1,0:T(8,128)(2,1)S(1)}, bf16[27,32,32]{2,1,0:T(8,128)(2,1)}, u32[]{:S(2)}) %copy-start) | copy-done | bytes 55320
  1.7 0.0 copy-start.1
  1.7 0.7 %copy-done.1 = bf16[1,64,64]{2,1,0:T(8,128)(2,1)S(1)} copy-done((bf16[1,64,64]{2,1,0:T(8,128)(2,1)S(1)}, bf16[1,64,64]{2,1,0:T(8,128)(2,1)}, u32[]{:S(2)}) %copy-start.1) | copy-done | bytes 8216
  2.4 0.0 copy-start.2
  2.4 0.7 %copy-done.2 = bf16[32,27]{1,0:T(8,128)(2,1)S(1)} copy-done((bf16[32,27]{1,0:T(8,128)(2,1)S(1)}, bf16[32,27]{1,0:T(8,128)(2,1)}, u32[]{:S(2)}) %copy-start.2) | copy-done | bytes 1752
  3.1 29.8 %shard_map.91 = f32[3,16,256]{2,1,0:T(8,128)S(1)} custom-call(bf16[1,64,64]{2,1,0:T(8,128)(2,1)S(1)} %copy-done.1, s32[1,64]{1,0:T(1,128)S(1)} %copy-done.4, s32[1,64]{1,0:T(1,128)S(1)} %copy-done.5, bf16[32,27]{1,0:T(8,128)(2,1)S(1)} %copy-done.2, f32[1,32]{1,0:T(1,128)S(1)} %bitcast.3, bf16[27,32,32]{2,1,0:T(8,128)(2,1)S(1)} %copy-done, ...), custom_call_target="tpu_custom_call" | custom-call | tf_op jit(solution)/shard_map/pallas_call | solution.py:373
  32.9 0.7 %reshape.16 = f32[1,1,3,4096]{3,1,2,0:T(1,128)} reshape(f32[3,16,256]{2,1,0:T(8,128)S(1)} %shard_map.91) | data formatting | bytes 98304 | tf_op jit(solution)/shard_map/reshape | solution.py:407
Async XLA Ops:
  0.0 0.7 %copy-start.5 = (s32[1,64]{1,0:T(1,128)S(1)}, s32[1,64]{1,0:T(1,128)}, u32[]{:S(2)}) copy-start(s32[1,64]{1,0:T(1,128)} %slot_ref.1) | copy-start | bytes 772
  0.0 0.7 %copy-start.6 = (f32[32]{0:T(128)S(1)}, f32[32]{0:T(128)}, u32[]{:S(2)}) copy-start(f32[32]{0:T(128)} %param.13) | copy-start | bytes 388
  0.0 0.7 %copy-start.7 = (f32[32]{0:T(128)S(1)}, f32[32]{0:T(128)}, u32[]{:S(2)}) copy-start(f32[32]{0:T(128)} %param.15) | copy-start | bytes 388
  0.0 0.7 %copy-start.8 = (f32[3]{0:T(128)S(1)}, f32[3]{0:T(128)}, u32[]{:S(2)}) copy-start(f32[3]{0:T(128)} %param.17) | copy-start | bytes 40
  0.0 0.7 %copy-start.3 = (bf16[3,32]{1,0:T(4,128)(2,1)S(1)}, bf16[3,32]{1,0:T(4,128)(2,1)}, u32[]{:S(2)}) copy-start(bf16[3,32]{1,0:T(4,128)(2,1)} %wh_ref.1) | copy-start | bytes 580
  0.0 0.7 %copy-start.4 = (s32[1,64]{1,0:T(1,128)S(1)}, s32[1,64]{1,0:T(1,128)}, u32[]{:S(2)}) copy-start(s32[1,64]{1,0:T(1,128)} %block_ref.1) | copy-start | bytes 772
  0.7 0.9 %copy-start = (bf16[27,32,32]{2,1,0:T(8,128)(2,1)S(1)}, bf16[27,32,32]{2,1,0:T(8,128)(2,1)}, u32[]{:S(2)}) copy-start(bf16[27,32,32]{2,1,0:T(8,128)(2,1)} %w2_ref.1) | copy-start | bytes 165892
  1.7 0.7 %copy-start.1 = (bf16[1,64,64]{2,1,0:T(8,128)(2,1)S(1)}, bf16[1,64,64]{2,1,0:T(8,128)(2,1)}, u32[]{:S(2)}) copy-start(bf16[1,64,64]{2,1,0:T(8,128)(2,1)} %em_ref.1) | copy-start | bytes 24580
  2.4 0.7 %copy-start.2 = (bf16[32,27]{1,0:T(8,128)(2,1)S(1)}, bf16[32,27]{1,0:T(8,128)(2,1)}, u32[]{:S(2)}) copy-start(bf16[32,27]{1,0:T(8,128)(2,1)} %w1_ref.1) | copy-start | bytes 5188

commit v2 on v1

--- a/solution.py
+++ b/solution.py
@@ -1,3 +1,5 @@
+import functools
+
 import jax
 import jax.numpy as jnp
 from jax import lax
@@ -9,6 +11,8 @@
 OVL = 6
 LANES = TILE * TILE
 C1 = 32
+SIDE = 8
+HUBS = 4
 AFF = 3
 MESH = pl.DeviceIdType.MESH
 F32 = jnp.float32
@@ -176,10 +180,10 @@
     em, block, slot, w1, b1, w2, b2, wh, bh,
     sent, arrived, expand, first, second, heads, hidden, partial,
     x_out, y_out, z_out, e_out, x_in, y_in, z_in, e_in,
-    load_sems, route_send, route_recv, swap_send, swap_recv,
+    load_sems, route_send, route_recv, swap_send, swap_recv, late_ready, all_ready,
 ):
     roll = pltpu.roll
-    blocks = 64
+    blocks = SIDE * SIDE
     me = lax.axis_index("blocks")
     own = lax.axis_index("octant")
     bits = [own % 2, own // 2 % 2, own // 4]
@@ -190,39 +194,25 @@
             total = total + (1 - bits[d] if mask >> d & 1 else bits[d]) * 2**d
         return total
 
-    barrier = pltpu.get_barrier_semaphore()
-
-    def greet(step, carry):
+    my, mz = me // SIDE, me % SIDE
+    early = mz < HUBS
+    spans = (4, 3, 5, 2, 6, 1, 7, 0)
+
+    def each_in(columns, visit):
+        for span in spans:
+            for z in columns:
+                target = (my + span) % SIDE * SIDE + z
+                if span:
+                    visit(target)
+                else:
+                    pl.when(mz != z)(functools.partial(visit, target))
+
+    def signal(semaphore, target):
         pl.semaphore_signal(
-            barrier, inc=1, device_id={"blocks": (me + step) % blocks}, device_id_type=MESH
+            semaphore, inc=1, device_id={"blocks": target}, device_id_type=MESH
         )
-        return carry
-
-    lax.fori_loop(1, blocks, greet, 0)
-    for mask in range(1, 8):
-        pl.semaphore_signal(
-            barrier, inc=1, device_id={"octant": partner(mask)}, device_id_type=MESH
-        )
-
-    loads = [
-        pltpu.make_async_copy(source, target, load_sems.at[index])
-        for index, (source, target) in enumerate(
-            [
-                (em_ref, em), (block_ref, block), (slot_ref, slot),
-                (w1_ref, w1), (b1_ref, b1), (w2_ref, w2), (b2_ref, b2), (wh_ref, wh), (bh_ref, bh),
-            ]
-        )
-    ]
-    for load in loads:
-        load.start()
-    for load in loads[:3]:
-        load.wait()
-    packed = pack_rows(em[0], block[...], slot[...])
-    sent[:, 0, :] = packed
-    pl.semaphore_wait(barrier, blocks - 1 + 7)
-
-    def send(step, carry):
-        target = (me + step) % blocks
+
+    def send(target):
         pltpu.make_async_remote_copy(
             src_ref=sent.at[target],
             dst_ref=arrived.at[me],
@@ -231,9 +221,46 @@
             device_id={"blocks": target},
             device_id_type=MESH,
         ).start()
-        return carry
-
-    lax.fori_loop(1, blocks, send, 0)
+
+    loads = [
+        pltpu.make_async_copy(source, target, load_sems.at[index])
+        for index, (source, target) in enumerate(
+            [
+                (block_ref, block), (slot_ref, slot), (em_ref, em),
+                (w1_ref, w1), (b1_ref, b1), (w2_ref, w2), (b2_ref, b2), (wh_ref, wh), (bh_ref, bh),
+            ]
+        )
+    ]
+    for load in loads:
+        load.start()
+    barrier = pltpu.get_barrier_semaphore()
+    for mask in range(1, 8):
+        pl.semaphore_signal(
+            barrier, inc=1, device_id={"octant": partner(mask)}, device_id_type=MESH
+        )
+    hub_columns, late_columns = range(HUBS), range(HUBS, SIDE)
+    hub_count, late_count = HUBS * SIDE, (SIDE - HUBS) * SIDE
+
+    @pl.when(early)
+    def _():
+        each_in(late_columns, functools.partial(signal, barrier))
+        each_in(hub_columns, functools.partial(signal, barrier))
+
+    @pl.when(jnp.logical_not(early))
+    def _():
+        pl.semaphore_wait(barrier, 7 + hub_count)
+        each_in(hub_columns, functools.partial(signal, late_ready))
+
+    for load in loads[:3]:
+        load.wait()
+    packed = pack_rows(em[0], block[...], slot[...])
+    sent[:, 0, :] = packed
+
+    @pl.when(early)
+    def _():
+        pl.semaphore_wait(barrier, 7 + hub_count - 1)
+
+    each_in(hub_columns, send)
     arrived[me] = sent[me]
 
     for load in loads[3:]:
@@ -259,6 +286,21 @@
     b2_col = column(b2[...])
     weights = blend_weights(bits)
 
+    @pl.when(early)
+    def _():
+        pl.semaphore_wait(late_ready, late_count)
+
+        @pl.when((mz == 0) | (mz == HUBS - 1))
+        def _():
+            first_told = my * SIDE + jnp.where(mz == 0, SIDE - 2, HUBS)
+            signal(all_ready, first_told)
+            signal(all_ready, first_told + 1)
+
+    @pl.when(jnp.logical_not(early))
+    def _():
+        pl.semaphore_wait(all_ready, 1)
+
+    each_in(late_columns, send)
     whole = pltpu.make_async_remote_copy(
         src_ref=sent.at[pl.ds(0, blocks - 1)],
         dst_ref=arrived.at[pl.ds(0, blocks - 1)],
@@ -291,26 +333,10 @@
     blended = jnp.stack(pieces, axis=0)
 
     tile = [[blended[:, 8 * hx : 8 * hx + 8, 128 * hy : 128 * hy + 128] for hy in range(2)] for hx in range(2)]
-    at_x = [move_x(tile[0][hy], tile[1][hy], bits[0], roll) for hy in range(2)]
-    at_y = [move_y(tile[hx][0], tile[hx][1], bits[1], roll) for hx in range(2)]
-    at_xy = move_y(at_x[0], at_x[1], bits[1], roll)
-    z_out[:, :8] = pack_z(tile[0][0], tile[0][1], bits[2], roll)
-    z_out[:, 8:] = pack_z(tile[1][0], tile[1][1], bits[2], roll)
-    x_out[:, :, :128] = at_x[0]
-    x_out[:, :, 128:] = at_x[1]
-    y_out[:, :8] = at_y[0]
-    y_out[:, 8:] = at_y[1]
-    e_out[0] = at_xy
-    e_out[1] = pack_z(at_x[0], at_x[1], bits[2], roll)
-    e_out[2] = pack_z(at_y[0], at_y[1], bits[2], roll)
-    e_out[3] = pack_z(at_xy, at_xy, bits[2], roll)
-
-    pairs = [
-        (4, z_out, z_in), (2, y_out, y_in), (6, e_out.at[2], e_in.at[2]), (7, e_out.at[3], e_in.at[3]),
-        (5, e_out.at[1], e_in.at[1]), (3, e_out.at[0], e_in.at[0]), (1, x_out, x_in),
-    ]
-    swaps = [
-        pltpu.make_async_remote_copy(
+    swaps = {}
+
+    def swap(mask, source, target):
+        swaps[mask] = pltpu.make_async_remote_copy(
             src_ref=source,
             dst_ref=target,
             send_sem=swap_send.at[mask - 1],
@@ -318,12 +344,28 @@
             device_id={"octant": partner(mask)},
             device_id_type=MESH,
         )
-        for mask, source, target in pairs
-    ]
-    for swap in swaps:
-        swap.start()
-    for swap in swaps:
-        swap.wait_recv()
+        swaps[mask].start()
+
+    z_out[:, :8] = pack_z(tile[0][0], tile[0][1], bits[2], roll)
+    z_out[:, 8:] = pack_z(tile[1][0], tile[1][1], bits[2], roll)
+    swap(4, z_out, z_in)
+    at_x = [move_x(tile[0][hy], tile[1][hy], bits[0], roll) for hy in range(2)]
+    e_out[1] = pack_z(at_x[0], at_x[1], bits[2], roll)
+    swap(5, e_out.at[1], e_in.at[1])
+    at_y = [move_y(tile[hx][0], tile[hx][1], bits[1], roll) for hx in range(2)]
+    y_out[:, :8] = at_y[0]
+    y_out[:, 8:] = at_y[1]
+    swap(2, y_out, y_in)
+    e_out[2] = pack_z(at_y[0], at_y[1], bits[2], roll)
+    swap(6, e_out.at[2], e_in.at[2])
+    at_xy = move_y(at_x[0], at_x[1], bits[1], roll)
+    e_out[0] = at_xy
+    swap(3, e_out.at[0], e_in.at[0])
+    e_out[3] = pack_z(at_xy, at_xy, bits[2], roll)
+    swap(7, e_out.at[3], e_in.at[3])
+    x_out[:, :, :128] = at_x[0]
+    x_out[:, :, 128:] = at_x[1]
+    swap(1, x_out, x_in)
 
     plane = [[tile[hx][hy] for hy in range(2)] for hx in range(2)]
 
@@ -333,34 +375,42 @@
     def is_half(bit, half, value):
         return jnp.where(bit == 1 - half, value, 0.0)
 
+    swaps[1].wait_recv()
     for hy in range(2):
         value = x_in[:, :, 128 * hy : 128 * hy + 128]
         for hx in range(2):
             add(hx, hy, is_half(bits[0], hx, value))
+    swaps[2].wait_recv()
     for hx in range(2):
         value = y_in[:, 8 * hx : 8 * hx + 8]
         for hy in range(2):
             add(hx, hy, is_half(bits[1], hy, value))
+    swaps[3].wait_recv()
+    swaps[7].wait_recv()
+    corner = e_in[0] + unpack_z(e_in[3], bits[2], roll)[0]
+    for hx in range(2):
+        for hy in range(2):
+            add(hx, hy, is_half(bits[0], hx, is_half(bits[1], hy, corner)))
+    swaps[6].wait_recv()
+    parts = unpack_z(e_in[2], bits[2], roll)
+    for hx in range(2):
+        for hy in range(2):
+            add(hx, hy, is_half(bits[1], hy, parts[hx]))
+    swaps[5].wait_recv()
+    parts = unpack_z(e_in[1], bits[2], roll)
+    for hx in range(2):
+        for hy in range(2):
+            add(hx, hy, is_half(bits[0], hx, parts[hy]))
+    swaps[4].wait_recv()
+    for hx in range(2):
         parts = unpack_z(z_in[:, 8 * hx : 8 * hx + 8], bits[2], roll)
         for hy in range(2):
             add(hx, hy, parts[hy])
-    corner = e_in[0] + unpack_z(e_in[3], bits[2], roll)[0]
-    for hx in range(2):
-        for hy in range(2):
-            add(hx, hy, is_half(bits[0], hx, is_half(bits[1], hy, corner)))
-    parts = unpack_z(e_in[1], bits[2], roll)
-    for hx in range(2):
-        for hy in range(2):
-            add(hx, hy, is_half(bits[0], hx, parts[hy]))
-    parts = unpack_z(e_in[2], bits[2], roll)
-    for hx in range(2):
-        for hy in range(2):
-            add(hx, hy, is_half(bits[1], hy, parts[hx]))
     for hx in range(2):
         for hy in range(2):
             out_ref[:, 8 * hx : 8 * hx + 8, 128 * hy : 128 * hy + 128] = plane[hx][hy]
-    for swap in swaps:
-        swap.wait_send()
+    for copy in swaps.values():
+        copy.wait_send()
     whole.wait_send()
 
 
@@ -399,9 +449,11 @@
             pltpu.SemaphoreType.DMA,
             pltpu.SemaphoreType.DMA((7,)),
             pltpu.SemaphoreType.DMA((7,)),
+            pltpu.SemaphoreType.REGULAR,
+            pltpu.SemaphoreType.REGULAR,
         ],
         compiler_params=pltpu.CompilerParams(
-            collective_id=0, has_side_effects=True, vmem_limit_bytes=32 * 1024 * 1024
+            collective_id=0, has_side_effects=True, vmem_limit_bytes=60 * 1024 * 1024
         ),
     )(*operands)
     return result.reshape(1, 1, AFF, TILE * LANES)

time: 33.8 us -> 29.3 us (0.87)
  local copies, waits for them, and re-layouts: 3.73 us -> 1.47 us
  Pallas kernels: 29.8 us -> 27.6 us
    unnamed x18 -> x0, local copies, waits for them, and re-layouts: 3.06 us -> none
    pallas_call x1, Pallas kernels: 29.8 us -> 27.6 us  [shards(): pl.pallas_call(kernel, out_shape=jax.ShapeDtypeStruct((AFF, TILE, LANES),...]
    reshape x1, local copies, waits for them, and re-layouts: 0.67 us -> 1.47 us  [shards(): return result.reshape(1, 1, AFF, TILE * LANES)]
where the time goes in v2:
time: 29.3 us; the launch traced here: 29.1 us
  Pallas kernels  27.6 us (94%)
  local copies, waits for them, and re-layouts  1.47 us (5%)
    pallas_call x1, Pallas kernels, shards(): pl.pallas_call(kernel, out_shape=jax.ShapeDtypeStruct((AFF, TILE, LANES),...  27.6 us
    reshape x1, local copies, waits for them, and re-layouts, shards(): return result.reshape(1, 1, AFF, TILE * LANES)  1.47 us

profile of v2, /device:TPU:1, one launch (start us, length us, event | category | flops | bytes accessed | tf_op | source)
XLA Modules:
  0.0 29.1 jit_solution(9018698817972921663)
XLA Ops:
  0.0 27.6 %shard_map.91 = f32[3,16,256]{2,1,0:T(8,128)} custom-call(bf16[1,64,64]{2,1,0:T(8,128)(2,1)} %em_ref.1, s32[1,64]{1,0:T(1,128)} %block_ref.1, s32[1,64]{1,0:T(1,128)} %slot_ref.1, bf16[32,27]{1,0:T(8,128)(2,1)} %w1_ref.1, f32[1,32]{1,0:T(1,128)} %bitcast.3, bf16[27,32,32]{2,1,0:T(8,128)(2,1)} %w2_ref.1, f32[1,32]{1,0:T(1,128)} %bitcast.4, ...), custom_call_target="tpu_custom_call" | custom-call | tf_op jit(solution)/shard_map/pallas_call | solution.py:423
  27.7 1.5 %reshape.16 = f32[1,1,3,4096]{3,1,2,0:T(1,128)} reshape(f32[3,16,256]{2,1,0:T(8,128)} %shard_map.91) | data formatting | bytes 98304 | tf_op jit(solution)/shard_map/reshape | solution.py:459

commit v3 on v2

--- a/solution.py
+++ b/solution.py
@@ -180,7 +180,8 @@
     em, block, slot, w1, b1, w2, b2, wh, bh,
     sent, arrived, expand, first, second, heads, hidden, partial,
     x_out, y_out, z_out, e_out, x_in, y_in, z_in, e_in,
-    load_sems, route_send, route_recv, swap_send, swap_recv, late_ready, all_ready,
+    load_sems, route_send, route_recv, swap_send, swap_recv,
+    relayed, relay_send, relay_recv, mate_ready,
 ):
     roll = pltpu.roll
     blocks = SIDE * SIDE
@@ -196,31 +197,50 @@
 
     my, mz = me // SIDE, me % SIDE
     early = mz < HUBS
+    half = HUBS * SIDE
+    slot_me = jnp.where(early, my * HUBS + mz, half + my * HUBS + mz - HUBS)
+    group_me = jnp.where(early, SIDE, my)
+    mate = my * SIDE + SIDE - 1 - mz
     spans = (4, 3, 5, 2, 6, 1, 7, 0)
-
-    def each_in(columns, visit):
-        for span in spans:
-            for z in columns:
-                target = (my + span) % SIDE * SIDE + z
-                if span:
-                    visit(target)
-                else:
-                    pl.when(mz != z)(functools.partial(visit, target))
 
     def signal(semaphore, target):
         pl.semaphore_signal(
             semaphore, inc=1, device_id={"blocks": target}, device_id_type=MESH
         )
 
-    def send(target):
-        pltpu.make_async_remote_copy(
-            src_ref=sent.at[target],
-            dst_ref=arrived.at[me],
-            send_sem=route_send,
-            recv_sem=route_recv,
-            device_id={"blocks": target},
+    def unless(condition, visit):
+        if condition is None:
+            visit()
+        else:
+            pl.when(jnp.logical_not(condition))(visit)
+
+    def greet(span, z):
+        target = (my + span) % SIDE * SIDE + z
+        unless(mz == z if span == 0 and z < HUBS else None, lambda: signal(barrier, target))
+
+    def rows(source, target, semaphores, device):
+        return pltpu.make_async_remote_copy(
+            src_ref=source,
+            dst_ref=target,
+            send_sem=semaphores[0],
+            recv_sem=semaphores[1],
+            device_id={"blocks": device},
             device_id_type=MESH,
-        ).start()
+        )
+
+    def send(span, z):
+        row = (my + span) % SIDE * SIDE
+        target = row + z
+        if z < HUBS:
+            device, place, semaphore = target, arrived, route_recv
+        else:
+            device, place, semaphore = row + SIDE - 1 - z, relayed, relay_recv.at[group_me]
+        copy = rows(sent.at[target], place.at[slot_me], (route_send, semaphore), device)
+        here = mz == (z if z < HUBS else SIDE - 1 - z)
+        unless(here if span == 0 else None, copy.start)
+
+    def landed(count, place, semaphores):
+        return rows(place.at[pl.ds(0, count)], place.at[pl.ds(0, count)], semaphores, mate)
 
     loads = [
         pltpu.make_async_copy(source, target, load_sems.at[index])
@@ -238,18 +258,17 @@
         pl.semaphore_signal(
             barrier, inc=1, device_id={"octant": partner(mask)}, device_id_type=MESH
         )
-    hub_columns, late_columns = range(HUBS), range(HUBS, SIDE)
-    hub_count, late_count = HUBS * SIDE, (SIDE - HUBS) * SIDE
 
     @pl.when(early)
     def _():
-        each_in(late_columns, functools.partial(signal, barrier))
-        each_in(hub_columns, functools.partial(signal, barrier))
+        for span in spans:
+            for z in range(SIDE):
+                greet(span, z)
 
     @pl.when(jnp.logical_not(early))
     def _():
-        pl.semaphore_wait(barrier, 7 + hub_count)
-        each_in(hub_columns, functools.partial(signal, late_ready))
+        pl.semaphore_wait(barrier, 7 + half)
+        signal(mate_ready, mate)
 
     for load in loads[:3]:
         load.wait()
@@ -258,10 +277,13 @@
 
     @pl.when(early)
     def _():
-        pl.semaphore_wait(barrier, 7 + hub_count - 1)
-
-    each_in(hub_columns, send)
-    arrived[me] = sent[me]
+        pl.semaphore_wait(barrier, 7 + half - 1)
+        arrived[slot_me] = sent[me]
+        relayed[slot_me] = sent[mate]
+
+    for span in spans:
+        for z in range(SIDE):
+            send(span, z)
 
     for load in loads[3:]:
         load.wait()
@@ -288,28 +310,21 @@
 
     @pl.when(early)
     def _():
-        pl.semaphore_wait(late_ready, late_count)
-
-        @pl.when((mz == 0) | (mz == HUBS - 1))
-        def _():
-            first_told = my * SIDE + jnp.where(mz == 0, SIDE - 2, HUBS)
-            signal(all_ready, first_told)
-            signal(all_ready, first_told + 1)
+        def forward(start, count, awaited, group):
+            landed(awaited, relayed, (relay_send, relay_recv.at[group])).wait_recv()
+            part = pl.ds(start, count)
+            rows(relayed.at[part], arrived.at[part], (relay_send, route_recv), mate).start()
+
+        pl.semaphore_wait(mate_ready, 1)
+        forward(0, half, half - 1, SIDE)
+        for y in (0, 1, 7, 2, 6, 3, 5, 4):
+            forward(half + y * HUBS, HUBS, HUBS, y)
+        landed(blocks - 1, arrived, (route_send, route_recv)).wait_recv()
 
     @pl.when(jnp.logical_not(early))
     def _():
-        pl.semaphore_wait(all_ready, 1)
-
-    each_in(late_columns, send)
-    whole = pltpu.make_async_remote_copy(
-        src_ref=sent.at[pl.ds(0, blocks - 1)],
-        dst_ref=arrived.at[pl.ds(0, blocks - 1)],
-        send_sem=route_send,
-        recv_sem=route_recv,
-        device_id={"blocks": (me + 1) % blocks},
-        device_id_type=MESH,
-    )
-    whole.wait_recv()
+        landed(blocks, arrived, (route_send, route_recv)).wait_recv()
+
     volume = unpack_volume(arrived[:, 0, :], expand[...])
     one = dot(first[...], conv1_columns(volume, roll)).reshape(TILE, C1, LANES)
     one = jnp.maximum(one + b1_col[None], 0.0).reshape(TILE * C1, LANES)
@@ -408,10 +423,18 @@
             add(hx, hy, parts[hy])
     for hx in range(2):
         for hy in range(2):
-            out_ref[:, 8 * hx : 8 * hx + 8, 128 * hy : 128 * hy + 128] = plane[hx][hy]
+            out_ref[:, pl.ds(TILE * hx + hy, 8, stride=2), :] = plane[hx][hy]
     for copy in swaps.values():
         copy.wait_send()
-    whole.wait_send()
+
+    @pl.when(early)
+    def _():
+        landed(blocks - 2, arrived, (route_send, route_recv)).wait_send()
+        landed(blocks, arrived, (relay_send, route_recv)).wait_send()
+
+    @pl.when(jnp.logical_not(early))
+    def _():
+        landed(blocks, arrived, (route_send, route_recv)).wait_send()
 
 
 def shards(em_store, route_block, route_slot, conv1_w, conv1_b, conv2_w, conv2_b, head_w, head_b):
@@ -419,11 +442,12 @@
         em_store, route_block, route_slot, conv1_w, conv1_b.reshape(1, C1), conv2_w,
         conv2_b.reshape(1, C1), head_w, head_b.reshape(1, AFF),
     )
+    operands = tuple(pltpu.with_memory_space_constraint(value, pltpu.HBM) for value in operands)
     vmem = pltpu.VMEM
     result = pl.pallas_call(
         kernel,
-        out_shape=jax.ShapeDtypeStruct((AFF, TILE, LANES), F32),
-        in_specs=[pl.BlockSpec(memory_space=pl.ANY)] * len(operands),
+        out_shape=jax.ShapeDtypeStruct((AFF, 2 * TILE, 128), F32),
+        in_specs=[pl.BlockSpec(memory_space=pltpu.HBM)] * len(operands),
         out_specs=pl.BlockSpec(memory_space=vmem),
         scratch_shapes=[vmem(value.shape, value.dtype) for value in operands]
         + [
@@ -449,11 +473,15 @@
             pltpu.SemaphoreType.DMA,
             pltpu.SemaphoreType.DMA((7,)),
             pltpu.SemaphoreType.DMA((7,)),
-            pltpu.SemaphoreType.REGULAR,
+        ]
+        + [
+            vmem((64, 1, 256), F32),
+            pltpu.SemaphoreType.DMA,
+            pltpu.SemaphoreType.DMA((SIDE + 1,)),
             pltpu.SemaphoreType.REGULAR,
         ],
         compiler_params=pltpu.CompilerParams(
-            collective_id=0, has_side_effects=True, vmem_limit_bytes=60 * 1024 * 1024
+            collective_id=0, has_side_effects=True, vmem_limit_bytes=32 * 1024 * 1024
         ),
     )(*operands)
     return result.reshape(1, 1, AFF, TILE * LANES)

time: 29.3 us -> 28 us (0.956)
  local copies, waits for them, and re-layouts: 1.47 us -> 0.62 us
  Pallas kernels: 27.6 us -> 27.3 us
    reshape x1 -> x0, local copies, waits for them, and re-layouts: 1.47 us -> none  [shards(): return result.reshape(1, 1, AFF, TILE * LANES)]
    unnamed x0 -> x1, local copies, waits for them, and re-layouts: none -> 0.62 us
    pallas_call x1, Pallas kernels: 27.6 us -> 27.3 us  [shards(): pl.pallas_call(kernel, out_shape=jax.ShapeDtypeStruct((AFF, 2 * TILE, 128...]
where the time goes in v3:
time: 28 us; the launch traced here: 27.9 us
  Pallas kernels  27.3 us (98%)
  local copies, waits for them, and re-layouts  0.62 us (2%)
    pallas_call x1, Pallas kernels, shards(): pl.pallas_call(kernel, out_shape=jax.ShapeDtypeStruct((AFF, 2 * TILE, 128...  27.3 us
    unnamed x1, local copies, waits for them, and re-layouts  0.62 us

profile of v3, /device:TPU:1, one launch (start us, length us, event | category | flops | bytes accessed | tf_op | source)
XLA Modules:
  0.0 27.9 jit_solution(5319372688483326037)
XLA Ops:
  0.0 27.3 %shard_map.91 = f32[3,32,128]{2,1,0:T(8,128)S(1)} custom-call(bf16[1,64,64]{2,1,0:T(8,128)(2,1)} %em_ref.1, s32[1,64]{1,0:T(1,128)} %block_ref.1, s32[1,64]{1,0:T(1,128)} %slot_ref.1, bf16[32,27]{1,0:T(8,128)(2,1)} %w1_ref.1, f32[1,32]{1,0:T(1,128)} %bitcast.5, bf16[27,32,32]{2,1,0:T(8,128)(2,1)} %w2_ref.1, f32[1,32]{1,0:T(1,128)} %bitcast.6, ...), custom_call_target="tpu_custom_call" | custom-call | tf_op jit(solution)/shard_map/pallas_call | solution.py:447
  27.3 0.6 %copy.13 = f32[1,1,3,4096]{3,1,2,0:T(1,128)} copy(f32[1,1,3,4096]{3,1,2,0:T(1,128)S(1)} %bitcast.4) | data formatting | bytes 98304

commit v4 on v3

--- a/solution.py
+++ b/solution.py
@@ -41,10 +41,9 @@
     slot_row = slots
     i_col = column((slot_row // 16 + 1).astype(F32))
     jk_col = column((slot_row % 16).astype(F32))
-    lane = iota((n, 128), 1)
-    spread = iota((64, 128), 0) == iota((64, 128), 1)
-    wide = dot(em, spread.astype(F32).astype(BF16))
-    wide = jnp.where(lane == 64, i_col, jnp.where(lane == 65, jk_col, wide)).astype(BF16)
+    lane = iota((n, 64), 1)
+    labels = jnp.where(lane == 0, i_col, jnp.where(lane == 1, jk_col, 0.0)).astype(BF16)
+    wide = jnp.concatenate([em, labels], axis=1)
     here = iota((64, n), 0).astype(F32) == target_row
     parts = [
         dot((here & (rank_row == rank)).astype(F32).astype(BF16), wide) for rank in (0.0, 1.0)
@@ -174,6 +173,20 @@
     return jnp.where(keep, head, 0.0), jnp.where(keep, tail, 0.0)
 
 
+def two_halves(first, second):
+    return jnp.concatenate([first, second], axis=1).astype(BF16)
+
+
+def edge(value):
+    upper = two_halves(value[0:1], value[1:2])
+    return jnp.concatenate([upper, two_halves(value[2:3], jnp.zeros_like(value[2:3]))], axis=0)
+
+
+def from_edge(ref):
+    value = ref[...].astype(F32)
+    return jnp.concatenate([value[0:1, :8], value[0:1, 8:], value[1:2, :8]], axis=0)
+
+
 def kernel(
     em_ref, block_ref, slot_ref, w1_ref, b1_ref, w2_ref, b2_ref, wh_ref, bh_ref,
     out_ref,
@@ -251,7 +264,7 @@
             ]
         )
     ]
-    for load in loads:
+    for load in loads[:3]:
         load.start()
     barrier = pltpu.get_barrier_semaphore()
     for mask in range(1, 8):
@@ -285,6 +298,8 @@
         for z in range(SIDE):
             send(span, z)
 
+    for load in loads[3:]:
+        load.start()
     for load in loads[3:]:
         load.wait()
     expand[...] = expander()
@@ -361,25 +376,24 @@
         )
         swaps[mask].start()
 
-    z_out[:, :8] = pack_z(tile[0][0], tile[0][1], bits[2], roll)
-    z_out[:, 8:] = pack_z(tile[1][0], tile[1][1], bits[2], roll)
+    z_out[...] = two_halves(
+        pack_z(tile[0][0], tile[0][1], bits[2], roll), pack_z(tile[1][0], tile[1][1], bits[2], roll)
+    )
     swap(4, z_out, z_in)
     at_x = [move_x(tile[0][hy], tile[1][hy], bits[0], roll) for hy in range(2)]
-    e_out[1] = pack_z(at_x[0], at_x[1], bits[2], roll)
+    e_out[1] = edge(pack_z(at_x[0], at_x[1], bits[2], roll))
     swap(5, e_out.at[1], e_in.at[1])
     at_y = [move_y(tile[hx][0], tile[hx][1], bits[1], roll) for hx in range(2)]
-    y_out[:, :8] = at_y[0]
-    y_out[:, 8:] = at_y[1]
+    y_out[...] = two_halves(at_y[0], at_y[1])
     swap(2, y_out, y_in)
-    e_out[2] = pack_z(at_y[0], at_y[1], bits[2], roll)
+    e_out[2] = edge(pack_z(at_y[0], at_y[1], bits[2], roll))
     swap(6, e_out.at[2], e_in.at[2])
     at_xy = move_y(at_x[0], at_x[1], bits[1], roll)
-    e_out[0] = at_xy
+    e_out[0] = edge(at_xy)
     swap(3, e_out.at[0], e_in.at[0])
-    e_out[3] = pack_z(at_xy, at_xy, bits[2], roll)
+    e_out[3] = edge(pack_z(at_xy, at_xy, bits[2], roll))
     swap(7, e_out.at[3], e_in.at[3])
-    x_out[:, :, :128] = at_x[0]
-    x_out[:, :, 128:] = at_x[1]
+    x_out[...] = two_halves(at_x[0], at_x[1])
     swap(1, x_out, x_in)
 
     plane = [[tile[hx][hy] for hy in range(2)] for hx in range(2)]
@@ -391,34 +405,37 @@
         return jnp.where(bit == 1 - half, value, 0.0)
 
     swaps[1].wait_recv()
+    face = x_in[...].astype(F32)
     for hy in range(2):
-        value = x_in[:, :, 128 * hy : 128 * hy + 128]
+        value = face[:, 8 * hy : 8 * hy + 8]
         for hx in range(2):
             add(hx, hy, is_half(bits[0], hx, value))
     swaps[2].wait_recv()
+    face = y_in[...].astype(F32)
     for hx in range(2):
-        value = y_in[:, 8 * hx : 8 * hx + 8]
+        value = face[:, 8 * hx : 8 * hx + 8]
         for hy in range(2):
             add(hx, hy, is_half(bits[1], hy, value))
     swaps[3].wait_recv()
     swaps[7].wait_recv()
-    corner = e_in[0] + unpack_z(e_in[3], bits[2], roll)[0]
+    corner = from_edge(e_in.at[0]) + unpack_z(from_edge(e_in.at[3]), bits[2], roll)[0]
     for hx in range(2):
         for hy in range(2):
             add(hx, hy, is_half(bits[0], hx, is_half(bits[1], hy, corner)))
     swaps[6].wait_recv()
-    parts = unpack_z(e_in[2], bits[2], roll)
+    parts = unpack_z(from_edge(e_in.at[2]), bits[2], roll)
     for hx in range(2):
         for hy in range(2):
             add(hx, hy, is_half(bits[1], hy, parts[hx]))
     swaps[5].wait_recv()
-    parts = unpack_z(e_in[1], bits[2], roll)
+    parts = unpack_z(from_edge(e_in.at[1]), bits[2], roll)
     for hx in range(2):
         for hy in range(2):
             add(hx, hy, is_half(bits[0], hx, parts[hy]))
     swaps[4].wait_recv()
+    face = z_in[...].astype(F32)
     for hx in range(2):
-        parts = unpack_z(z_in[:, 8 * hx : 8 * hx + 8], bits[2], roll)
+        parts = unpack_z(face[:, 8 * hx : 8 * hx + 8], bits[2], roll)
         for hy in range(2):
             add(hx, hy, parts[hy])
     for hx in range(2):
@@ -461,10 +478,10 @@
             vmem((TILE, 3, C1, LANES), F32),
         ]
         + [
-            vmem((AFF, 8, 256), F32),
-            vmem((AFF, 16, 128), F32),
-            vmem((AFF, 16, 128), F32),
-            vmem((4, AFF, 8, 128), F32),
+            vmem((AFF, 16, 128), BF16),
+            vmem((AFF, 16, 128), BF16),
+            vmem((AFF, 16, 128), BF16),
+            vmem((4, 2, 16, 128), BF16),
         ]
         * 2
         + [

time: 28 us -> 28 us (level)
  no operation moved by 1% of the time
where the time goes in v4:
time: 28 us; the launch traced here: 27.7 us
  Pallas kernels  27.1 us (97%)
  local copies, waits for them, and re-layouts  0.62 us (2%)
    pallas_call x1, Pallas kernels, shards(): pl.pallas_call(kernel, out_shape=jax.ShapeDtypeStruct((AFF, 2 * TILE, 128...  27.1 us
    unnamed x1, local copies, waits for them, and re-layouts  0.62 us

profile of v4, /device:TPU:1, one launch (start us, length us, event | category | flops | bytes accessed | tf_op | source)
XLA Modules:
  0.0 27.7 jit_solution(15103193826743280732)
XLA Ops:
  0.0 27.1 %shard_map.91 = f32[3,32,128]{2,1,0:T(8,128)S(1)} custom-call(bf16[1,64,64]{2,1,0:T(8,128)(2,1)} %em_ref.1, s32[1,64]{1,0:T(1,128)} %block_ref.1, s32[1,64]{1,0:T(1,128)} %slot_ref.1, bf16[32,27]{1,0:T(8,128)(2,1)} %w1_ref.1, f32[1,32]{1,0:T(1,128)} %bitcast.5, bf16[27,32,32]{2,1,0:T(8,128)(2,1)} %w2_ref.1, f32[1,32]{1,0:T(1,128)} %bitcast.6, ...), custom_call_target="tpu_custom_call" | custom-call | tf_op jit(solution)/shard_map/pallas_call | solution.py:464
  27.1 0.6 %copy.13 = f32[1,1,3,4096]{3,1,2,0:T(1,128)} copy(f32[1,1,3,4096]{3,1,2,0:T(1,128)S(1)} %bitcast.4) | data formatting | bytes 98304

commit v5 on v3

--- a/solution.py
+++ b/solution.py
@@ -12,7 +12,8 @@
 LANES = TILE * TILE
 C1 = 32
 SIDE = 8
-HUBS = 4
+HUBS = 3
+RELAYS = {7: (0, 0), 6: (1, 0), 5: (2, 0), 4: (1, 1), 3: (0, 1)}
 AFF = 3
 MESH = pl.DeviceIdType.MESH
 F32 = jnp.float32
@@ -41,10 +42,9 @@
     slot_row = slots
     i_col = column((slot_row // 16 + 1).astype(F32))
     jk_col = column((slot_row % 16).astype(F32))
-    lane = iota((n, 128), 1)
-    spread = iota((64, 128), 0) == iota((64, 128), 1)
-    wide = dot(em, spread.astype(F32).astype(BF16))
-    wide = jnp.where(lane == 64, i_col, jnp.where(lane == 65, jk_col, wide)).astype(BF16)
+    lane = iota((n, 64), 1)
+    labels = jnp.where(lane == 0, i_col, jnp.where(lane == 1, jk_col, 0.0)).astype(BF16)
+    wide = jnp.concatenate([em, labels], axis=1)
     here = iota((64, n), 0).astype(F32) == target_row
     parts = [
         dot((here & (rank_row == rank)).astype(F32).astype(BF16), wide) for rank in (0.0, 1.0)
@@ -181,7 +181,7 @@
     sent, arrived, expand, first, second, heads, hidden, partial,
     x_out, y_out, z_out, e_out, x_in, y_in, z_in, e_in,
     load_sems, route_send, route_recv, swap_send, swap_recv,
-    relayed, relay_send, relay_recv, mate_ready,
+    relayed, relay_send, relay_recv, mate_ready, mates_ready, partners_told,
 ):
     roll = pltpu.roll
     blocks = SIDE * SIDE
@@ -197,11 +197,15 @@
 
     my, mz = me // SIDE, me % SIDE
     early = mz < HUBS
-    half = HUBS * SIDE
-    slot_me = jnp.where(early, my * HUBS + mz, half + my * HUBS + mz - HUBS)
+    twice = mz < 2
+    hubs, others = HUBS * SIDE, SIDE - HUBS
+    slot_me = jnp.where(early, my * HUBS + mz, hubs + my * others + mz - HUBS)
     group_me = jnp.where(early, SIDE, my)
-    mate = my * SIDE + SIDE - 1 - mz
+    pupils = [my * SIDE + SIDE - 1 - mz, my * SIDE + HUBS + mz]
+    relay = my * SIDE + jnp.where(mz >= SIDE - HUBS, SIDE - 1 - mz, mz - HUBS)
+    lane_me = jnp.where(mz >= SIDE - HUBS, 0, 1)
     spans = (4, 3, 5, 2, 6, 1, 7, 0)
+    rows_first = (0, 1, 7, 2, 6, 3, 5, 4)
 
     def signal(semaphore, target):
         pl.semaphore_signal(
@@ -228,19 +232,19 @@
             device_id_type=MESH,
         )
 
-    def send(span, z):
-        row = (my + span) % SIDE * SIDE
-        target = row + z
+    def send(y, z):
+        target = y * SIDE + z
         if z < HUBS:
             device, place, semaphore = target, arrived, route_recv
         else:
-            device, place, semaphore = row + SIDE - 1 - z, relayed, relay_recv.at[group_me]
+            hub, lane = RELAYS[z]
+            device, place = y * SIDE + hub, relayed.at[lane]
+            semaphore = relay_recv.at[lane, group_me]
         copy = rows(sent.at[target], place.at[slot_me], (route_send, semaphore), device)
-        here = mz == (z if z < HUBS else SIDE - 1 - z)
-        unless(here if span == 0 else None, copy.start)
+        unless(me == device, copy.start)
 
     def landed(count, place, semaphores):
-        return rows(place.at[pl.ds(0, count)], place.at[pl.ds(0, count)], semaphores, mate)
+        return rows(place.at[pl.ds(0, count)], place.at[pl.ds(0, count)], semaphores, (me + 1) % blocks)
 
     loads = [
         pltpu.make_async_copy(source, target, load_sems.at[index])
@@ -251,24 +255,23 @@
             ]
         )
     ]
-    for load in loads:
+    for load in loads[:3]:
         load.start()
     barrier = pltpu.get_barrier_semaphore()
-    for mask in range(1, 8):
-        pl.semaphore_signal(
-            barrier, inc=1, device_id={"octant": partner(mask)}, device_id_type=MESH
-        )
+
+    def greet_partners(semaphore):
+        for mask in range(1, 8):
+            pl.semaphore_signal(
+                semaphore, inc=1, device_id={"octant": partner(mask)}, device_id_type=MESH
+            )
+
 
     @pl.when(early)
     def _():
+        greet_partners(barrier)
         for span in spans:
             for z in range(SIDE):
                 greet(span, z)
-
-    @pl.when(jnp.logical_not(early))
-    def _():
-        pl.semaphore_wait(barrier, 7 + half)
-        signal(mate_ready, mate)
 
     for load in loads[:3]:
         load.wait()
@@ -277,14 +280,22 @@
 
     @pl.when(early)
     def _():
-        pl.semaphore_wait(barrier, 7 + half - 1)
+        pl.semaphore_wait(barrier, 7 + hubs - 1)
         arrived[slot_me] = sent[me]
-        relayed[slot_me] = sent[mate]
-
-    for span in spans:
+        relayed[0, slot_me] = sent[pupils[0]]
+        relayed[1, slot_me] = sent[pupils[1]]
+
+    @pl.when(jnp.logical_not(early))
+    def _():
+        pl.semaphore_wait(barrier, hubs)
+        signal(mate_ready.at[lane_me], relay)
+
+    for y in rows_first:
         for z in range(SIDE):
-            send(span, z)
-
+            send(y, z)
+
+    for load in loads[3:]:
+        load.start()
     for load in loads[3:]:
         load.wait()
     expand[...] = expander()
@@ -308,17 +319,35 @@
     b2_col = column(b2[...])
     weights = blend_weights(bits)
 
+    def forward(lane, start, count, awaited, group):
+        landed(awaited, relayed.at[lane], (relay_send, relay_recv.at[lane, group])).wait_recv()
+        part = pl.ds(start, count)
+        rows(
+            relayed.at[lane, part], arrived.at[part], (relay_send, route_recv), pupils[lane]
+        ).start()
+
+    def begin(lane):
+        pl.semaphore_wait(mate_ready.at[lane], 1)
+        greet_partners(mates_ready.at[lane])
+        forward(lane, 0, hubs, hubs - 1, SIDE)
+
+    def finish(lane):
+        pl.semaphore_wait(mates_ready.at[lane], 7)
+        signal(partners_told, pupils[lane])
+
+    def also(visit, *numbers):
+        pl.when(twice)(functools.partial(visit, 1, *numbers))
+
     @pl.when(early)
     def _():
-        def forward(start, count, awaited, group):
-            landed(awaited, relayed, (relay_send, relay_recv.at[group])).wait_recv()
-            part = pl.ds(start, count)
-            rows(relayed.at[part], arrived.at[part], (relay_send, route_recv), mate).start()
-
-        pl.semaphore_wait(mate_ready, 1)
-        forward(0, half, half - 1, SIDE)
-        for y in (0, 1, 7, 2, 6, 3, 5, 4):
-            forward(half + y * HUBS, HUBS, HUBS, y)
+        also(begin)
+        begin(0)
+        for y in rows_first:
+            group = (hubs + y * others, others, others, y)
+            forward(0, *group)
+            also(forward, *group)
+        finish(0)
+        also(finish)
         landed(blocks - 1, arrived, (route_send, route_recv)).wait_recv()
 
     @pl.when(jnp.logical_not(early))
@@ -348,6 +377,10 @@
     blended = jnp.stack(pieces, axis=0)
 
     tile = [[blended[:, 8 * hx : 8 * hx + 8, 128 * hy : 128 * hy + 128] for hy in range(2)] for hx in range(2)]
+    @pl.when(jnp.logical_not(early))
+    def _():
+        pl.semaphore_wait(partners_told, 1)
+
     swaps = {}
 
     def swap(mask, source, target):
@@ -429,8 +462,16 @@
 
     @pl.when(early)
     def _():
-        landed(blocks - 2, arrived, (route_send, route_recv)).wait_send()
+        landed(blocks - 3, arrived, (route_send, route_recv)).wait_send()
         landed(blocks, arrived, (relay_send, route_recv)).wait_send()
+
+    @pl.when(twice)
+    def _():
+        landed(blocks, arrived, (relay_send, route_recv)).wait_send()
+
+    @pl.when(mz == HUBS - 1)
+    def _():
+        landed(1, arrived, (route_send, route_recv)).wait_send()
 
     @pl.when(jnp.logical_not(early))
     def _():
@@ -475,9 +516,11 @@
             pltpu.SemaphoreType.DMA((7,)),
         ]
         + [
-            vmem((64, 1, 256), F32),
+            vmem((2, 64, 1, 256), F32),
             pltpu.SemaphoreType.DMA,
-            pltpu.SemaphoreType.DMA((SIDE + 1,)),
+            pltpu.SemaphoreType.DMA((2, SIDE + 1)),
+            pltpu.SemaphoreType.REGULAR((2,)),
+            pltpu.SemaphoreType.REGULAR((2,)),
             pltpu.SemaphoreType.REGULAR,
         ],
         compiler_params=pltpu.CompilerParams(

time: 28 us -> 27.4 us (0.979)
  Pallas kernels: 27.3 us -> 26.5 us
    pallas_call x1, Pallas kernels: 27.3 us -> 26.5 us  [shards(): pl.pallas_call(kernel, out_shape=jax.ShapeDtypeStruct((AFF, 2 * TILE, 128...]
where the time goes in v5:
time: 27.4 us; the launch traced here: 27.2 us
  Pallas kernels  26.5 us (97%)
  local copies, waits for them, and re-layouts  0.62 us (2%)
    pallas_call x1, Pallas kernels, shards(): pl.pallas_call(kernel, out_shape=jax.ShapeDtypeStruct((AFF, 2 * TILE, 128...  26.5 us
    unnamed x1, local copies, waits for them, and re-layouts  0.62 us

profile of v5, /device:TPU:1, one launch (start us, length us, event | category | flops | bytes accessed | tf_op | source)
XLA Modules:
  0.0 27.2 jit_solution(14783665645408057447)
XLA Ops:
  0.0 26.5 %shard_map.91 = f32[3,32,128]{2,1,0:T(8,128)S(1)} custom-call(bf16[1,64,64]{2,1,0:T(8,128)(2,1)} %em_ref.1, s32[1,64]{1,0:T(1,128)} %block_ref.1, s32[1,64]{1,0:T(1,128)} %slot_ref.1, bf16[32,27]{1,0:T(8,128)(2,1)} %w1_ref.1, f32[1,32]{1,0:T(1,128)} %bitcast.5, bf16[27,32,32]{2,1,0:T(8,128)(2,1)} %w2_ref.1, f32[1,32]{1,0:T(1,128)} %bitcast.6, ...), custom_call_target="tpu_custom_call" | custom-call | tf_op jit(solution)/shard_map/pallas_call | solution.py:488
  26.5 0.6 %copy.13 = f32[1,1,3,4096]{3,1,2,0:T(1,128)} copy(f32[1,1,3,4096]{3,1,2,0:T(1,128)S(1)} %bitcast.4) | data formatting | bytes 98304

commit v6 on v5

--- a/solution.py
+++ b/solution.py
@@ -53,9 +53,9 @@
 
 
 def expander():
-    row = iota((128, 4 * LANES), 0)
-    col = iota((128, 4 * LANES), 1)
-    wanted = (col // LANES) * 16 + (col // 16 % 4) * 4 + col % 4
+    row = iota((128, 4 * 128), 0)
+    col = iota((128, 4 * 128), 1)
+    wanted = (col // 128) * 16 + (col // 16 % 4) * 4 + col % 4
     return (row == wanted).astype(F32).astype(BF16)
 
 
@@ -72,7 +72,8 @@
     x_row = iota((TILE, 128), 0)
     volume = jnp.zeros((TILE, LANES), F32)
     for a in range(4):
-        masked = jnp.where(inside, spread[:, a * LANES : (a + 1) * LANES], 0.0).astype(BF16)
+        part = spread[:, a * 128 : a * 128 + 128]
+        masked = jnp.where(inside, jnp.concatenate([part, part], axis=1), 0.0).astype(BF16)
         wanted = (x_row % 4 == a) & ((x_row // 4 + 1).astype(F32) == i_row)
         volume = volume + dot(wanted.astype(F32).astype(BF16), masked)
     return volume
@@ -116,11 +117,11 @@
     return jnp.concatenate(rows, axis=0).astype(BF16)
 
 
-def z_shifted(half, roll):
-    z = iota(half.shape, 1) % TILE
-    before = jnp.where(z > 0, shift_lanes(half, -1, roll), 0.0)
-    after = jnp.where(z < TILE - 1, shift_lanes(half, 1, roll), 0.0)
-    return jnp.concatenate([before, half, after], axis=0).astype(BF16)
+def z_shifted(value, roll):
+    z = iota(value.shape, 1) % TILE
+    before = jnp.where(z > 0, shift_lanes(value, -1, roll), 0.0)
+    after = jnp.where(z < TILE - 1, shift_lanes(value, 1, roll), 0.0)
+    return [part.astype(BF16) for part in (before, value, after)]
 
 
 def head_matrix(head_w):
@@ -300,20 +301,22 @@
         load.wait()
     expand[...] = expander()
     first[...] = first_matrix(w1[...])
-    wide = replicated(w2[...].reshape(27 * C1, C1), 8)
-    x_inner = iota((C1, 8 * C1), 1) // C1
-    for x in range(10):
+    wide = replicated(w2[...].reshape(27 * C1, C1), 2)
+    x_inner = iota((C1, 2 * C1), 1) // C1
+    for x in range(4):
         for dy in range(3):
+            columns = []
             for dz in range(3):
-                block_rows = jnp.zeros((C1, 8 * C1), F32)
+                block_rows = jnp.zeros((C1, 2 * C1), F32)
                 for dx in range(3):
-                    if 0 <= x + dx - 2 < 8:
+                    if 0 <= x + dx - 2 < 2:
                         at = (9 * dx + 3 * dy + dz) * C1
                         block_rows = jnp.where(
                             x_inner == x + dx - 2, wide[at : at + C1], block_rows
                         )
-                at = (x * 3 + dy) * C1
-                second[at : at + C1, dz * 256 : dz * 256 + 256] = block_rows.astype(BF16)
+                columns.append(block_rows)
+            at = (x * 3 + dy) * C1
+            second[at : at + C1, :] = jnp.concatenate(columns, axis=1).astype(BF16)
     heads[...] = head_matrix(wh[...])
     b1_col = column(b1[...])
     b2_col = column(b2[...])
@@ -357,14 +360,18 @@
     volume = unpack_volume(arrived[:, 0, :], expand[...])
     one = dot(first[...], conv1_columns(volume, roll)).reshape(TILE, C1, LANES)
     one = jnp.maximum(one + b1_col[None], 0.0).reshape(TILE * C1, LANES)
-    for h in range(2):
-        hidden[h] = z_shifted(one[h * 256 : h * 256 + 256], roll)
-    low = dot(second[3 * C1 : 30 * C1], hidden[0]).reshape(9, 3, C1, LANES)
-    high = dot(second[: 27 * C1], hidden[1]).reshape(9, 3, C1, LANES)
-    both = low[7:] + high[:2]
-    partial[:7] = low[:7]
-    partial[7:9] = both
-    partial[9:] = high[2:]
+    for dz, part in enumerate(z_shifted(one, roll)):
+        hidden[:, dz] = part.reshape(8, 2 * C1, LANES)
+    held = None
+    for group in range(8):
+        sums = dot(second[...], hidden[group].reshape(6 * C1, LANES)).reshape(4, 3, C1, LANES)
+        if held is None:
+            partial[0] = sums[1]
+        else:
+            partial[2 * group - 1] = held[0] + sums[0]
+            partial[2 * group] = held[1] + sums[1]
+        held = sums[2:]
+    partial[TILE - 1] = held[0]
     y = iota((1, 1, LANES), 2) // TILE
     total = partial[:, 1]
     total = total + jnp.where(y > 0, shift_lanes(partial[:, 0].reshape(512, LANES), -TILE, roll).reshape(TILE, C1, LANES), 0.0)
@@ -494,11 +501,11 @@
         + [
             vmem((64, 1, 256), F32),
             vmem((64, 1, 256), F32),
-            vmem((128, 4 * LANES), BF16),
+            vmem((128, 4 * 128), BF16),
             vmem((TILE * C1, LANES), BF16),
-            vmem((30 * C1, 3 * 256), BF16),
+            vmem((12 * C1, 6 * C1), BF16),
             vmem((AFF * TILE, TILE * C1), BF16),
-            vmem((2, 768, LANES), BF16),
+            vmem((8, 3, 2 * C1, LANES), BF16),
             vmem((TILE, 3, C1, LANES), F32),
         ]
         + [

time: 27.4 us -> 27 us (0.985)
  Pallas kernels: 26.5 us -> 26.1 us
    pallas_call x1, Pallas kernels: 26.5 us -> 26.1 us  [shards(): pl.pallas_call(kernel, out_shape=jax.ShapeDtypeStruct((AFF, 2 * TILE, 128...]
where the time goes in v6:
time: 27 us; the launch traced here: 26.8 us
  Pallas kernels  26.1 us (97%)
  local copies, waits for them, and re-layouts  0.62 us (2%)
    pallas_call x1, Pallas kernels, shards(): pl.pallas_call(kernel, out_shape=jax.ShapeDtypeStruct((AFF, 2 * TILE, 128...  26.1 us
    unnamed x1, local copies, waits for them, and re-layouts  0.62 us

profile of v6, /device:TPU:1, one launch (start us, length us, event | category | flops | bytes accessed | tf_op | source)
XLA Modules:
  0.0 26.8 jit_solution(9841405898548221593)
XLA Ops:
  0.0 26.1 %shard_map.91 = f32[3,32,128]{2,1,0:T(8,128)S(1)} custom-call(bf16[1,64,64]{2,1,0:T(8,128)(2,1)} %em_ref.1, s32[1,64]{1,0:T(1,128)} %block_ref.1, s32[1,64]{1,0:T(1,128)} %slot_ref.1, bf16[32,27]{1,0:T(8,128)(2,1)} %w1_ref.1, f32[1,32]{1,0:T(1,128)} %bitcast.5, bf16[27,32,32]{2,1,0:T(8,128)(2,1)} %w2_ref.1, f32[1,32]{1,0:T(1,128)} %bitcast.6, ...), custom_call_target="tpu_custom_call" | custom-call | tf_op jit(solution)/shard_map/pallas_call | solution.py:495
  26.1 0.6 %copy.13 = f32[1,1,3,4096]{3,1,2,0:T(1,128)} copy(f32[1,1,3,4096]{3,1,2,0:T(1,128)S(1)} %bitcast.4) | data formatting | bytes 98304

commit v7 on v6

--- a/solution.py
+++ b/solution.py
@@ -118,10 +118,11 @@
 
 
 def z_shifted(value, roll):
-    z = iota(value.shape, 1) % TILE
-    before = jnp.where(z > 0, shift_lanes(value, -1, roll), 0.0)
-    after = jnp.where(z < TILE - 1, shift_lanes(value, 1, roll), 0.0)
-    return [part.astype(BF16) for part in (before, value, after)]
+    z = iota((1, LANES), 1) % TILE
+    value = value.astype(BF16)
+    before = shift_lanes(value, -1, roll) * jnp.where(z > 0, 1.0, 0.0).astype(BF16)
+    after = shift_lanes(value, 1, roll) * jnp.where(z < TILE - 1, 1.0, 0.0).astype(BF16)
+    return [before, value, after]
 
 
 def head_matrix(head_w):
@@ -256,8 +257,6 @@
             ]
         )
     ]
-    for load in loads[:3]:
-        load.start()
     barrier = pltpu.get_barrier_semaphore()
 
     def greet_partners(semaphore):
@@ -269,11 +268,13 @@
 
     @pl.when(early)
     def _():
+        for span in spans:
+            for z in (6, 5, 7, 4, 0, 3, 1, 2):
+                greet(span, z)
         greet_partners(barrier)
-        for span in spans:
-            for z in range(SIDE):
-                greet(span, z)
-
+
+    for load in loads[:3]:
+        load.start()
     for load in loads[:3]:
         load.wait()
     packed = pack_rows(em[0], block[...], slot[...])
@@ -349,15 +350,18 @@
             group = (hubs + y * others, others, others, y)
             forward(0, *group)
             also(forward, *group)
+        landed(blocks - 1, arrived, (route_send, route_recv)).wait_recv()
+
+    @pl.when(jnp.logical_not(early))
+    def _():
+        landed(blocks, arrived, (route_send, route_recv)).wait_recv()
+
+    volume = unpack_volume(arrived[:, 0, :], expand[...])
+    @pl.when(early)
+    def _():
         finish(0)
         also(finish)
-        landed(blocks - 1, arrived, (route_send, route_recv)).wait_recv()
-
-    @pl.when(jnp.logical_not(early))
-    def _():
-        landed(blocks, arrived, (route_send, route_recv)).wait_recv()
-
-    volume = unpack_volume(arrived[:, 0, :], expand[...])
+
     one = dot(first[...], conv1_columns(volume, roll)).reshape(TILE, C1, LANES)
     one = jnp.maximum(one + b1_col[None], 0.0).reshape(TILE * C1, LANES)
     for dz, part in enumerate(z_shifted(one, roll)):

time: 27 us -> 27.1 us (level)
  no operation moved by 1% of the time
where the time goes in v7:
time: 27.1 us; the launch traced here: 26.8 us
  Pallas kernels  26.2 us (97%)
  local copies, waits for them, and re-layouts  0.62 us (2%)
    pallas_call x1, Pallas kernels, shards(): pl.pallas_call(kernel, out_shape=jax.ShapeDtypeStruct((AFF, 2 * TILE, 128...  26.2 us
    unnamed x1, local copies, waits for them, and re-layouts  0.62 us

profile of v7, /device:TPU:1, one launch (start us, length us, event | category | flops | bytes accessed | tf_op | source)
XLA Modules:
  0.0 26.8 jit_solution(16572246202962909818)
XLA Ops:
  0.0 26.2 %shard_map.91 = f32[3,32,128]{2,1,0:T(8,128)S(1)} custom-call(bf16[1,64,64]{2,1,0:T(8,128)(2,1)} %em_ref.1, s32[1,64]{1,0:T(1,128)} %block_ref.1, s32[1,64]{1,0:T(1,128)} %slot_ref.1, bf16[32,27]{1,0:T(8,128)(2,1)} %w1_ref.1, f32[1,32]{1,0:T(1,128)} %bitcast.5, bf16[27,32,32]{2,1,0:T(8,128)(2,1)} %w2_ref.1, f32[1,32]{1,0:T(1,128)} %bitcast.6, ...), custom_call_target="tpu_custom_call" | custom-call | tf_op jit(solution)/shard_map/pallas_call | solution.py:499
  26.2 0.6 %copy.13 = f32[1,1,3,4096]{3,1,2,0:T(1,128)} copy(f32[1,1,3,4096]{3,1,2,0:T(1,128)S(1)} %bitcast.4) | data formatting | bytes 98304

commit v8 on v7

--- a/solution.py
+++ b/solution.py
@@ -45,11 +45,9 @@
     lane = iota((n, 64), 1)
     labels = jnp.where(lane == 0, i_col, jnp.where(lane == 1, jk_col, 0.0)).astype(BF16)
     wide = jnp.concatenate([em, labels], axis=1)
-    here = iota((64, n), 0).astype(F32) == target_row
-    parts = [
-        dot((here & (rank_row == rank)).astype(F32).astype(BF16), wide) for rank in (0.0, 1.0)
-    ]
-    return jnp.concatenate(parts, axis=1)
+    row = iota((128, n), 0)
+    here = ((row % 64).astype(F32) == target_row) & ((row // 64).astype(F32) == rank_row)
+    return dot(here.astype(F32).astype(BF16), wide)
 
 
 def expander():
@@ -180,7 +178,7 @@
     em_ref, block_ref, slot_ref, w1_ref, b1_ref, w2_ref, b2_ref, wh_ref, bh_ref,
     out_ref,
     em, block, slot, w1, b1, w2, b2, wh, bh,
-    sent, arrived, expand, first, second, heads, hidden, partial,
+    sent, arrived, expand, first, second, heads, hidden, two,
     x_out, y_out, z_out, e_out, x_in, y_in, z_in, e_in,
     load_sems, route_send, route_recv, swap_send, swap_recv,
     relayed, relay_send, relay_recv, mate_ready, mates_ready, partners_told,
@@ -278,7 +276,8 @@
     for load in loads[:3]:
         load.wait()
     packed = pack_rows(em[0], block[...], slot[...])
-    sent[:, 0, :] = packed
+    sent[:, 0, :128] = packed[:64]
+    sent[:, 0, 128:] = packed[64:]
 
     @pl.when(early)
     def _():
@@ -366,22 +365,25 @@
     one = jnp.maximum(one + b1_col[None], 0.0).reshape(TILE * C1, LANES)
     for dz, part in enumerate(z_shifted(one, roll)):
         hidden[:, dz] = part.reshape(8, 2 * C1, LANES)
+    y = iota((1, LANES), 1) // TILE
+
+    def complete(x, sums):
+        total = sums[1]
+        total = total + jnp.where(y > 0, shift_lanes(sums[0], -TILE, roll), 0.0)
+        total = total + jnp.where(y < TILE - 1, shift_lanes(sums[2], TILE, roll), 0.0)
+        two[x * C1 : x * C1 + C1, :] = jnp.maximum(total + b2_col, 0.0).astype(BF16)
+
     held = None
     for group in range(8):
         sums = dot(second[...], hidden[group].reshape(6 * C1, LANES)).reshape(4, 3, C1, LANES)
         if held is None:
-            partial[0] = sums[1]
+            complete(0, sums[1])
         else:
-            partial[2 * group - 1] = held[0] + sums[0]
-            partial[2 * group] = held[1] + sums[1]
+            complete(2 * group - 1, held[0] + sums[0])
+            complete(2 * group, held[1] + sums[1])
         held = sums[2:]
-    partial[TILE - 1] = held[0]
-    y = iota((1, 1, LANES), 2) // TILE
-    total = partial[:, 1]
-    total = total + jnp.where(y > 0, shift_lanes(partial[:, 0].reshape(512, LANES), -TILE, roll).reshape(TILE, C1, LANES), 0.0)
-    total = total + jnp.where(y < TILE - 1, shift_lanes(partial[:, 2].reshape(512, LANES), TILE, roll).reshape(TILE, C1, LANES), 0.0)
-    two = jnp.maximum(total + b2_col[None], 0.0).reshape(TILE * C1, LANES).astype(BF16)
-    logits = dot(heads[...], two)
+    complete(TILE - 1, held[0])
+    logits = dot(heads[...], two[...])
     pieces = []
     for a in range(AFF):
         pieces.append(jax.nn.sigmoid(logits[a * TILE : a * TILE + TILE] + bh[:, a : a + 1]) * weights)
@@ -510,7 +512,7 @@
             vmem((12 * C1, 6 * C1), BF16),
             vmem((AFF * TILE, TILE * C1), BF16),
             vmem((8, 3, 2 * C1, LANES), BF16),
-            vmem((TILE, 3, C1, LANES), F32),
+            vmem((TILE * C1, LANES), BF16),
         ]
         + [
             vmem((AFF, 8, 256), F32),

time: 27.1 us -> 27.1 us (level)
  no operation moved by 1% of the time
where the time goes in v8:
time: 27.1 us; the launch traced here: 26.8 us
  Pallas kernels  26.2 us (97%)
  local copies, waits for them, and re-layouts  0.62 us (2%)
    pallas_call x1, Pallas kernels, shards(): pl.pallas_call(kernel, out_shape=jax.ShapeDtypeStruct((AFF, 2 * TILE, 128...  26.2 us
    unnamed x1, local copies, waits for them, and re-layouts  0.62 us

profile of v8, /device:TPU:1, one launch (start us, length us, event | category | flops | bytes accessed | tf_op | source)
XLA Modules:
  0.0 26.8 jit_solution(17249779390458130550)
XLA Ops:
  0.0 26.2 %shard_map.91 = f32[3,32,128]{2,1,0:T(8,128)S(1)} custom-call(bf16[1,64,64]{2,1,0:T(8,128)(2,1)} %em_ref.1, s32[1,64]{1,0:T(1,128)} %block_ref.1, s32[1,64]{1,0:T(1,128)} %slot_ref.1, bf16[32,27]{1,0:T(8,128)(2,1)} %w1_ref.1, f32[1,32]{1,0:T(1,128)} %bitcast.5, bf16[27,32,32]{2,1,0:T(8,128)(2,1)} %w2_ref.1, f32[1,32]{1,0:T(1,128)} %bitcast.6, ...), custom_call_target="tpu_custom_call" | custom-call | tf_op jit(solution)/shard_map/pallas_call | solution.py:501
  26.2 0.6 %copy.13 = f32[1,1,3,4096]{3,1,2,0:T(1,128)} copy(f32[1,1,3,4096]{3,1,2,0:T(1,128)S(1)} %bitcast.4) | data formatting | bytes 98304

commit v9 on v8

--- a/solution.py
+++ b/solution.py
@@ -407,23 +407,23 @@
         )
         swaps[mask].start()
 
+    at_x = [move_x(tile[0][hy], tile[1][hy], bits[0], roll) for hy in range(2)]
+    e_out[1] = pack_z(at_x[0], at_x[1], bits[2], roll)
+    swap(5, e_out.at[1], e_in.at[1])
+    at_xy = move_y(at_x[0], at_x[1], bits[1], roll)
+    e_out[3] = pack_z(at_xy, at_xy, bits[2], roll)
+    swap(7, e_out.at[3], e_in.at[3])
     z_out[:, :8] = pack_z(tile[0][0], tile[0][1], bits[2], roll)
     z_out[:, 8:] = pack_z(tile[1][0], tile[1][1], bits[2], roll)
     swap(4, z_out, z_in)
-    at_x = [move_x(tile[0][hy], tile[1][hy], bits[0], roll) for hy in range(2)]
-    e_out[1] = pack_z(at_x[0], at_x[1], bits[2], roll)
-    swap(5, e_out.at[1], e_in.at[1])
     at_y = [move_y(tile[hx][0], tile[hx][1], bits[1], roll) for hx in range(2)]
+    e_out[2] = pack_z(at_y[0], at_y[1], bits[2], roll)
+    swap(6, e_out.at[2], e_in.at[2])
     y_out[:, :8] = at_y[0]
     y_out[:, 8:] = at_y[1]
     swap(2, y_out, y_in)
-    e_out[2] = pack_z(at_y[0], at_y[1], bits[2], roll)
-    swap(6, e_out.at[2], e_in.at[2])
-    at_xy = move_y(at_x[0], at_x[1], bits[1], roll)
     e_out[0] = at_xy
     swap(3, e_out.at[0], e_in.at[0])
-    e_out[3] = pack_z(at_xy, at_xy, bits[2], roll)
-    swap(7, e_out.at[3], e_in.at[3])
     x_out[:, :, :128] = at_x[0]
     x_out[:, :, 128:] = at_x[1]
     swap(1, x_out, x_in)

time: 27.1 us -> 26.5 us (0.978)
  Pallas kernels: 26.2 us -> 25.6 us
    pallas_call x1, Pallas kernels: 26.2 us -> 25.6 us  [shards(): pl.pallas_call(kernel, out_shape=jax.ShapeDtypeStruct((AFF, 2 * TILE, 128...]
where the time goes in v9:
time: 26.5 us; the launch traced here: 26.2 us
  Pallas kernels  25.6 us (97%)
  local copies, waits for them, and re-layouts  0.62 us (2%)
    pallas_call x1, Pallas kernels, shards(): pl.pallas_call(kernel, out_shape=jax.ShapeDtypeStruct((AFF, 2 * TILE, 128...  25.6 us
    unnamed x1, local copies, waits for them, and re-layouts  0.62 us

profile of v9, /device:TPU:1, one launch (start us, length us, event | category | flops | bytes accessed | tf_op | source)
XLA Modules:
  0.0 26.2 jit_solution(17056877562173249949)
XLA Ops:
  0.0 25.6 %shard_map.91 = f32[3,32,128]{2,1,0:T(8,128)S(1)} custom-call(bf16[1,64,64]{2,1,0:T(8,128)(2,1)} %em_ref.1, s32[1,64]{1,0:T(1,128)} %block_ref.1, s32[1,64]{1,0:T(1,128)} %slot_ref.1, bf16[32,27]{1,0:T(8,128)(2,1)} %w1_ref.1, f32[1,32]{1,0:T(1,128)} %bitcast.5, bf16[27,32,32]{2,1,0:T(8,128)(2,1)} %w2_ref.1, f32[1,32]{1,0:T(1,128)} %bitcast.6, ...), custom_call_target="tpu_custom_call" | custom-call | tf_op jit(solution)/shard_map/pallas_call | solution.py:501
  25.6 0.6 %copy.13 = f32[1,1,3,4096]{3,1,2,0:T(1,128)} copy(f32[1,1,3,4096]{3,1,2,0:T(1,128)S(1)} %bitcast.4) | data formatting | bytes 98304

commit v10 on v9

--- a/solution.py
+++ b/solution.py
@@ -413,17 +413,17 @@
     at_xy = move_y(at_x[0], at_x[1], bits[1], roll)
     e_out[3] = pack_z(at_xy, at_xy, bits[2], roll)
     swap(7, e_out.at[3], e_in.at[3])
+    e_out[0] = at_xy
+    swap(3, e_out.at[0], e_in.at[0])
+    at_y = [move_y(tile[hx][0], tile[hx][1], bits[1], roll) for hx in range(2)]
+    e_out[2] = pack_z(at_y[0], at_y[1], bits[2], roll)
+    swap(6, e_out.at[2], e_in.at[2])
     z_out[:, :8] = pack_z(tile[0][0], tile[0][1], bits[2], roll)
     z_out[:, 8:] = pack_z(tile[1][0], tile[1][1], bits[2], roll)
     swap(4, z_out, z_in)
-    at_y = [move_y(tile[hx][0], tile[hx][1], bits[1], roll) for hx in range(2)]
-    e_out[2] = pack_z(at_y[0], at_y[1], bits[2], roll)
-    swap(6, e_out.at[2], e_in.at[2])
     y_out[:, :8] = at_y[0]
     y_out[:, 8:] = at_y[1]
     swap(2, y_out, y_in)
-    e_out[0] = at_xy
-    swap(3, e_out.at[0], e_in.at[0])
     x_out[:, :, :128] = at_x[0]
     x_out[:, :, 128:] = at_x[1]
     swap(1, x_out, x_in)

time: 26.5 us -> 26.5 us (level)
  no operation moved by 1% of the time
where the time goes in v10:
time: 26.5 us; the launch traced here: 26.2 us
  Pallas kernels  25.6 us (97%)
  local copies, waits for them, and re-layouts  0.62 us (2%)
    pallas_call x1, Pallas kernels, shards(): pl.pallas_call(kernel, out_shape=jax.ShapeDtypeStruct((AFF, 2 * TILE, 128...  25.6 us
    unnamed x1, local copies, waits for them, and re-layouts  0.62 us

profile of v10, /device:TPU:1, one launch (start us, length us, event | category | flops | bytes accessed | tf_op | source)
XLA Modules:
  0.0 26.2 jit_solution(10797161211417899335)
XLA Ops:
  0.0 25.6 %shard_map.91 = f32[3,32,128]{2,1,0:T(8,128)S(1)} custom-call(bf16[1,64,64]{2,1,0:T(8,128)(2,1)} %em_ref.1, s32[1,64]{1,0:T(1,128)} %block_ref.1, s32[1,64]{1,0:T(1,128)} %slot_ref.1, bf16[32,27]{1,0:T(8,128)(2,1)} %w1_ref.1, f32[1,32]{1,0:T(1,128)} %bitcast.5, bf16[27,32,32]{2,1,0:T(8,128)(2,1)} %w2_ref.1, f32[1,32]{1,0:T(1,128)} %bitcast.6, ...), custom_call_target="tpu_custom_call" | custom-call | tf_op jit(solution)/shard_map/pallas_call | solution.py:501
  25.6 0.6 %copy.13 = f32[1,1,3,4096]{3,1,2,0:T(1,128)} copy(f32[1,1,3,4096]{3,1,2,0:T(1,128)S(1)} %bitcast.4) | data formatting | bytes 98304
